TPU v7x, 128 devices: a whole 4x4x4 slice. The times are simulated.
128 devices in a mesh: freq: 4 (over y), space: 32 (over x, z, core).
Axes of the slice: x: 4, y: 4, z: 4, core: 2. Of those that a mesh axis runs over, the one named last changes fastest.
Arguments:
- boundary_power_density: bfloat16 [32, 524288], P(None, ('freq', 'space')), may hold values from -6 to 6
- face_scales: bfloat16 [524288], P(('freq', 'space')), may hold values from 0.5 to 5
- face_node: int32 [524288], P(('freq', 'space')), may hold values from 0 to 511
- send_counts: int32 [4096], P(('freq', 'space')), may hold values from 1 to 128, as said below
- tile_values: bfloat16 [4096, 8, 128, 128], P('space')
- tile_mask: int32 [4096, 8], P('space'), may hold values from 0 to 1, as said below
- tile_columns: int32 [4096, 8], P('space'), may hold values from 0 to 135, as said below
- film_sink: float32 [524288], P('space'), may hold values from 0.01 to 0.2
- capacity: float32 [524288], P('space'), may hold values from 0.1 to 1
Outputs:
- surface_harmonics: float32 [32, 65536], P('freq', 'space')
- temperature: float32 [32, 524288], P('freq', 'space')
Inputs may be any that keep to these rules, and one draw needn't show every extreme that they name: `send_counts`: every fluid device sends exactly 128 live slots to one partition, the same for all fluid devices in a draw. `tile_mask`: slot 0 of each row tile is live. `tile_columns`: row tile r of a partition (counted in it) names distinct extended tiles of r to r + 8, slot 0 naming r + 4.
All inputs are finite; a program needn't handle non-finite values.
Results may differ from a plain program's by a relative error of at most 0.0011.
Values may be sent and summed in bfloat16 or wider, within the bound.
No kernel may reach another device: no remote copies, remote signals or barrier semaphores. Data moves between devices by JAX's collectives and lax.ppermute only.
A program may use at most 128 MiB of HBM per device.

v0:
```python
import math

import jax
import jax.numpy as jnp
from jax import lax
from jax.sharding import PartitionSpec as P

BOUNDARY_PER_CPU = 512
HALO_TILES = 4
SWEEPS = 8


LOW_EDGE = 0.05
HIGH_EDGE = 2.0
FREQUENCY_SPACING = 0.003


def extended_2(shard, sides, width):
    for axis, dim in sides:
        size, length = (lax.axis_size(axis), shard.shape[dim])
        up = [(i, (i + 1) % size) for i in range(size - 1)]
        down = [(j, i) for i, j in up]
        last = lax.slice_in_dim(shard, length - width, length, axis=dim)
        first = lax.slice_in_dim(shard, 0, width, axis=dim)
        before = lax.ppermute(last, axis, up)
        after = lax.ppermute(first, axis, down)
        shard = jnp.concatenate([before, shard, after], axis=dim)
    return shard


def fourier_matrix(thermal_states):
    harmonic_part = jnp.arange(thermal_states, dtype=jnp.int32)
    position_couple = (harmonic_part // 2).astype(jnp.float32)
    parity = harmonic_part % 2
    instant_grid = jnp.arange(thermal_states, dtype=jnp.int32).astype(jnp.float32)
    cycle_argument = (
        2.0 * math.pi / thermal_states * position_couple[:, None] * instant_grid[None, :]
    )
    cosine_vector = jnp.where(
        position_couple[:, None] == 0,
        1.0 / thermal_states,
        2.0 / thermal_states * jnp.cos(cycle_argument),
    )
    odd_wave_weights = jnp.where(
        position_couple[:, None] == 0,
        jnp.cos(math.pi * instant_grid)[None, :] / thermal_states,
        -2.0 / thermal_states * jnp.sin(cycle_argument),
    )
    return jnp.where(parity[:, None] == 1, odd_wave_weights, cosine_vector)


def rotate(vector_in):
    halves = vector_in.reshape(vector_in.shape[0] // 2, 2, vector_in.shape[1])
    return jnp.stack([-halves[:, 1], halves[:, 0]], axis=1).reshape(vector_in.shape)


def couple(extended, columns, mask_bf, tiles, rows_count, tile_size, nodes_count):
    blocks = extended.reshape(rows_count, extended.shape[1] // tile_size, tile_size)
    picked = blocks[:, columns] * mask_bf[None, :, :, None]
    coupled = jnp.einsum("crtj,rtij->cri", picked, tiles, preferred_element_type=jnp.float32)
    return coupled.reshape(rows_count, nodes_count)


def chebyshev(rhs, diagonal, apply):
    centre = 0.5 * (HIGH_EDGE + LOW_EDGE)
    half_width = 0.5 * (HIGH_EDGE - LOW_EDGE)
    stretch = centre / half_width
    previous = 1.0 / stretch
    solution = jnp.zeros(rhs.shape, jnp.float32)
    residual = rhs
    direction = residual / (centre * diagonal[None, :])
    for sweep in range(SWEEPS):
        solution = solution + direction
        if sweep + 1 < SWEEPS:
            residual = residual - apply(direction)
            current = 1.0 / (2.0 * stretch - previous)
            direction = (
                current * previous * direction
                + 2.0 * current / half_width * residual / diagonal[None, :]
            )
            previous = current
    return solution


def local(
    boundary_power_density,
    face_scales,
    face_node,
    send_counts,
    tile_values,
    tile_mask,
    tile_columns,
    film_sink,
    capacity,
):
    spatial_extent = lax.axis_size("space")
    cluster_total = lax.axis_size("freq")
    thermal_states, opening_total = boundary_power_density.shape
    frequency_bin = opening_total // spatial_extent
    slot_index = jnp.arange(opening_total, dtype=jnp.int32)
    send_limit = jnp.repeat(send_counts, frequency_bin, total_repeat_length=opening_total)
    weight = jnp.where(
        slot_index % frequency_bin < send_limit, face_scales, jnp.zeros_like(face_scales)
    )
    target = slot_index // frequency_bin * BOUNDARY_PER_CPU + face_node
    weighted = boundary_power_density.astype(jnp.float32) * weight.astype(jnp.float32)[None, :]
    dense_sums = (
        jnp.zeros((thermal_states, spatial_extent * BOUNDARY_PER_CPU), jnp.float32)
        .at[:, target]
        .add(weighted)
    )
    level_sums = lax.psum_scatter(dense_sums, "space", scatter_dimension=1, tiled=True)
    resident_lines = thermal_states // cluster_total
    fourier_lines = fourier_matrix(thermal_states)
    group_index = lax.axis_index("freq")
    nodes_here = film_sink.shape[0]
    tile_size = tile_values.shape[2]
    row_tiles = nodes_here // tile_size
    rim_width = HALO_TILES * tile_size
    gathered = lax.all_gather(level_sums, "freq", axis=1, tiled=True)
    rows_here = lax.dynamic_slice_in_dim(
        fourier_lines, group_index * resident_lines, resident_lines, 0
    )
    surface = jnp.dot(rows_here, gathered, precision=lax.Precision.HIGHEST)
    rhs = jnp.pad(surface, ((0, 0), (0, nodes_here - surface.shape[1])))
    mask_bf = tile_mask.astype(jnp.bfloat16)
    spread = jnp.broadcast_to(mask_bf[:, :, None], (row_tiles, tile_mask.shape[1], tile_size))
    rowsum = jnp.einsum(
        "rtij,rtj->ri", tile_values, spread, preferred_element_type=jnp.float32
    ).reshape(nodes_here)
    diagonal = rowsum + film_sink
    first_comp = group_index * resident_lines
    strength = FREQUENCY_SPACING * (
        (first_comp + jnp.arange(resident_lines, dtype=jnp.int32)) // 2
    ).astype(jnp.float32)

    def apply_components(vector_in):
        rounded = vector_in.astype(jnp.bfloat16)
        extended = extended_2(rounded, (("space", 1),), rim_width)
        coupled = couple(
            extended, tile_columns, mask_bf, tile_values, resident_lines, tile_size, nodes_here
        )
        return (
            diagonal[None, :] * vector_in
            - coupled
            + strength[:, None] * capacity[None, :] * rotate(vector_in)
        )

    solution = chebyshev(rhs, diagonal, apply_components)
    return (surface, solution)


def solution(mesh):
    placed = (
        P(None, ("freq", "space")),
        P(("freq", "space")),
        P(("freq", "space")),
        P(("freq", "space")),
        P("space", None, None, None),
        P("space", None),
        P("space", None),
        P("space"),
        P("space"),
    )
    return jax.shard_map(
        local,
        mesh=mesh,
        in_specs=placed,
        out_specs=(P("freq", "space"), P("freq", "space")),
        check_vma=False,
    )
```

profile of v0, /device:TPU:97, one launch (start us, length us, event | category | flops | bytes accessed | tf_op | source)
XLA Modules:
  0.0 399.6 jit_solution(11527356446139688623)
XLA Ops:
  7.2 1.8 fusion.100
  9.1 2.1 fusion.99
  11.2 4.4 %compare_select_fusion.1 = (s32[4096,1]{0,1:T(1,128)S(1)}, s32[4096,1]{0,1:T(1,128)S(1)}) fusion(s32[]{:T(128)} %bitcast.29, s32[]{:T(128)} %bitcast.30, s32[]{:T(128)} %bitcast.31, s32[]{:T(128)} %bitcast.32, s32[]{:T(128)} %bitcast.33, s32[]{:T(128)} %bitcast.35, s32[]{:T(128)} %bitcast.34, s32[4096,1]{0,1:T(1,128)S(1)} %bitcast.229, ...), kind=kLoop, calls=%fused_computation.127 | loop fusion | flops 57344 | bytes 65564 | tf_op jit(solution)/shard_map/jit(_take)/gather | solution.py:101
  15.6 1.2 compare_reduce_fusion.24
  16.8 16.5 %fusion.63 = f32[4096]{0:T(1024)S(1)} fusion(bf16[4096]{0:T(1024)(128)(2,1)} %param.12, pred[4096]{0:T(1024)(128)(4,1)S(1)} %get-tuple-element.38, pred[4096]{0:T(1024)(128)(4,1)S(1)} %get-tuple-element.37, pred[4096]{0:T(1024)(128)(4,1)S(1)} %get-tuple-element.36, pred[4096]{0:T(1024)(128)(4,1)S(1)} %get-tuple-element.35, ...), kind=kLoop, calls=%fused_computation.156 | loop fusion | flops 176128 | bytes 143460 | tf_op jit(solution)/shard_map/convert_element_type | solution.py:106
  33.3 1.0 multiply_bitcast_fusion
  34.3 0.6 copy.14
  34.9 26.1 %scatter_custom_fusion = f32[32,16384]{0,1:T(8,128)} fusion(s32[4096]{0:T(1024)S(1)} %compare_select_fusion.8, f32[4096,32]{1,0:T(8,128)S(1)} %copy.14, f32[]{:T(128)} %constant.177.clone.1), kind=kCustom, calls=%fused_computation.40 | custom fusion | flops 131072 | bytes 2097156 | tf_op jit(solution)/shard_map/scatter-add | solution.py:110
  61.0 0.6 copy-done.22
  62.3 14.6 %fusion.48 = f32[128,1,128,1]{2,1,3,0:T(1,128)S(1)} fusion(bf16[128,8,128,128]{3,2,1,0:T(8,128)(2,1)} %param.15, bf16[128,8]{1,0:T(8,128)(2,1)S(1)} %copy.27), kind=kOutput, calls=%fused_computation.99 | convolution fusion | flops 33554432 | bytes 33622016 | tf_op jit(solution)/shard_map/rtij,rtj->ri/dot_general | solution.py:128
  77.0 75.9 %reduce-scatter.2.cloned.1.call-done = f32[32,512]{0,1:T(8,128)} async-done(((f32[32,16384]{0,1:T(8,128)}), f32[32,512]{0,1:T(8,128)}) %reduce-scatter.2.cloned.1.call-update) | async-done | bytes 65552 | tf_op jit(solution)/shard_map/reduce_scatter | solution.py:112
  152.9 12.4 %all_gather.3 = f32[32,2048]{0,1:T(8,128)S(1)} all-gather(f32[32,512]{0,1:T(8,128)} %reduce-scatter.2.cloned.1.call-done), channel_id=1, replica_groups=mesh['freq'=4,'space'=32] {'freq'}, dimensions={1}, use_global_device_ids=true | all-gather | bytes 327680 | tf_op jit(solution)/shard_map/all_gather | solution.py:120
  165.3 1.0 fusion.67
  166.4 8.5 %collective-permute-start = (bf16[8,512]{1,0:T(8,128)(2,1)S(1)}, bf16[8,512]{1,0:T(8,128)(2,1)S(1)}, u32[]{:S(2)}, u32[]{:S(2)}) collective-permute-start(bf16[8,512]{1,0:T(8,128)(2,1)S(1)} %get-tuple-element.81), channel_id=1, source_target_pairs={{0,1},{1,2},{2,3},{3,4},{4,5},{5,6},{6,7},{7,8},{8,9},{9,10},{10,1... | collective-permute-start | bytes 24584 | tf_op jit(solution)/shard_map/ppermute | solution.py:25
  174.9 1.9 collective-permute-start.1
  177.2 0.4 slice_negate_fusion.6
  177.6 0.5 pad_maximum_fusion
  178.4 3.6 collective-permute-done.1
  182.0 3.3 gather_fusion
  185.4 15.2 %fusion.91 = (bf16[8,16384]{1,0:T(8,128)(2,1)S(1)}, f32[8,16384]{1,0:T(8,128)S(1)}, f32[8,16384]{1,0:T(8,128)}) fusion(f32[16384]{0:T(1024)S(1)} %get-tuple-element.52, f32[16384]{0:T(1024)S(1)} %get-tuple-element.51, f32[8,2048]{1,0:T(8,128)S(1)} %fusion.67, f32[8,16384]{1,0:T(8,128)S(1)} %reshape.244, f32[16384]{0:T(1024)S(1)} %copy-done.4, ...), kind=kOutput, calls=%fused_computation.199 | convolution fusion | flops 271056896 | bytes 37750816 | tf_op jit(solution)/shard_map/crtj,rtij->cri/dot_general | solution.py:60
  200.6 2.2 collective-permute-start.2
  202.8 2.3 collective-permute-start.3
  205.4 0.4 slice_negate_fusion.5
  205.8 0.5 pad_maximum_fusion.1
  206.3 1.1 reshape.248
  207.5 2.4 collective-permute-done.3
  209.9 3.3 gather_fusion.1
  213.2 15.5 %fusion.90 = (bf16[8,16384]{1,0:T(8,128)(2,1)S(1)}, f32[8,16384]{1,0:T(8,128)S(1)}, f32[8,16384]{1,0:T(8,128)}) fusion(f32[16384]{0:T(1024)S(1)} %get-tuple-element.52, f32[8,16384]{1,0:T(8,128)S(1)} %get-tuple-element.50, f32[8,16384]{1,0:T(8,128)} %get-tuple-element.117, f32[8,16384]{1,0:T(8,128)} %reshape.248, f32[16384]{0:T(1024)S(1)} %copy-done.4, ...), kind=kOutput, calls=%fused_computation.198 | convolution fusion | flops 270925824 | bytes 38668320 | tf_op jit(solution)/shard_map/crtj,rtij->cri/dot_general | solution.py:60
  228.7 3.2 collective-permute-start.4
  231.9 1.9 collective-permute-start.5
  234.6 0.5 pad_maximum_fusion.2
  235.4 3.5 collective-permute-done.5
  239.0 7.6 %gather_fusion.2 = bf16[1024,8,128]{2,1,0:T(8,128)(2,1)} fusion(bf16[8,136,128]{2,0,1:T(8,128)(2,1)S(1)} %maximum_bitcast_fusion.2, s32[1024]{0:T(1024)S(1)} %broadcast_clamp_fusion), kind=kCustom, calls=%fused_computation.2 | custom fusion | bytes 4198400 | tf_op jit(solution)/shard_map/gather | solution.py:59
  246.6 15.0 %fusion.89 = (bf16[8,16384]{1,0:T(8,128)(2,1)S(1)}, f32[8,16384]{1,0:T(8,128)S(1)}, f32[8,16384]{1,0:T(8,128)S(1)}) fusion(f32[16384]{0:T(1024)S(1)} %get-tuple-element.52, f32[8,16384]{1,0:T(8,128)S(1)} %get-tuple-element.48, f32[8,16384]{1,0:T(8,128)S(1)} %copy-done.5, f32[8,16384]{1,0:T(8,128)S(1)} %reshape.252, f32[16384]{0:T(1024)S(1)} %copy-done.4, ...), kind=kOutput, calls=%fused_computation.197 | convolution fusion | flops 270925824 | bytes 38668320 | tf_op jit(solution)/shard_map/crtj,rtij->cri/dot_general | solution.py:60
  261.6 2.2 collective-permute-start.6
  263.9 2.1 collective-permute-start.7
  266.7 0.5 pad_maximum_fusion.3
  267.2 1.2 reshape.256
  268.4 2.6 collective-permute-done.7
  271.0 7.6 %gather_fusion.3 = bf16[1024,8,128]{2,1,0:T(8,128)(2,1)} fusion(bf16[8,136,128]{2,0,1:T(8,128)(2,1)S(1)} %maximum_bitcast_fusion.3, s32[1024]{0:T(1024)S(1)} %broadcast_clamp_fusion), kind=kCustom, calls=%fused_computation.3 | custom fusion | bytes 4198400 | tf_op jit(solution)/shard_map/gather | solution.py:59
  278.6 15.0 %fusion.88 = (bf16[8,16384]{1,0:T(8,128)(2,1)S(1)}, f32[8,16384]{1,0:T(8,128)S(1)}, f32[8,16384]{1,0:T(8,128)S(1)}) fusion(f32[16384]{0:T(1024)S(1)} %get-tuple-element.52, f32[8,16384]{1,0:T(8,128)S(1)} %get-tuple-element.46, f32[8,16384]{1,0:T(8,128)S(1)} %get-tuple-element.119, f32[8,16384]{1,0:T(8,128)} %reshape.256, f32[16384]{0:T(1024)S(1)} %copy-done.4, ...), kind=kOutput, calls=%fused_computation.196 | convolution fusion | flops 270925824 | bytes 38668320 | tf_op jit(solution)/shard_map/crtj,rtij->cri/dot_general | solution.py:60
  293.6 3.0 collective-permute-start.8
  296.7 2.1 collective-permute-start.9
  299.1 0.4 slice_negate_fusion.2
  299.6 0.5 pad_maximum_fusion.4
  300.0 1.2 reshape.260
  301.2 2.5 collective-permute-done.9
  303.8 7.6 %gather_fusion.4 = bf16[1024,8,128]{2,1,0:T(8,128)(2,1)} fusion(bf16[8,136,128]{2,0,1:T(8,128)(2,1)S(1)} %maximum_bitcast_fusion.4, s32[1024]{0:T(1024)S(1)} %broadcast_clamp_fusion), kind=kCustom, calls=%fused_computation.4 | custom fusion | bytes 4198400 | tf_op jit(solution)/shard_map/gather | solution.py:59
  311.4 15.8 %fusion.87 = (bf16[8,16384]{1,0:T(8,128)(2,1)S(1)}, f32[8,16384]{1,0:T(8,128)S(1)}, f32[8,16384]{1,0:T(8,128)}) fusion(f32[16384]{0:T(1024)S(1)} %get-tuple-element.52, f32[8,16384]{1,0:T(8,128)S(1)} %get-tuple-element.44, f32[8,16384]{1,0:T(8,128)S(1)} %get-tuple-element.120, f32[8,16384]{1,0:T(8,128)} %reshape.260, f32[16384]{0:T(1024)S(1)} %copy-done.4, ...), kind=kOutput, calls=%fused_computation.195 | convolution fusion | flops 270925824 | bytes 38668320 | tf_op jit(solution)/shard_map/crtj,rtij->cri/dot_general | solution.py:60
  327.2 3.2 collective-permute-start.10
  330.4 1.9 collective-permute-start.11
  333.1 0.5 pad_maximum_fusion.5
  333.5 1.2 reshape.264
  334.7 2.8 collective-permute-done.11
  337.5 1.0 maximum_bitcast_fusion.5
  338.5 7.6 %gather_fusion.5 = bf16[1024,8,128]{2,1,0:T(8,128)(2,1)} fusion(bf16[8,136,128]{2,0,1:T(8,128)(2,1)S(1)} %maximum_bitcast_fusion.5, s32[1024]{0:T(1024)S(1)} %broadcast_clamp_fusion), kind=kCustom, calls=%fused_computation.5 | custom fusion | bytes 4198400 | tf_op jit(solution)/shard_map/gather | solution.py:59
  346.1 15.9 %fusion.86 = (bf16[8,16384]{1,0:T(8,128)(2,1)}, f32[8,16384]{1,0:T(8,128)S(1)}, f32[8,16384]{1,0:T(8,128)}) fusion(f32[16384]{0:T(1024)S(1)} %get-tuple-element.52, f32[8,16384]{1,0:T(8,128)S(1)} %get-tuple-element.42, f32[8,16384]{1,0:T(8,128)S(1)} %copy-done.6, f32[8,16384]{1,0:T(8,128)} %reshape.264, f32[16384]{0:T(1024)S(1)} %copy-done.4, ...), kind=kOutput, calls=%fused_computation.194 | convolution fusion | flops 270925824 | bytes 38668320 | tf_op jit(solution)/shard_map/crtj,rtij->cri/dot_general | solution.py:60
  363.1 3.0 collective-permute-start.12
  366.1 1.9 collective-permute-start.13
  368.0 0.5 pad_maximum_fusion.6
  368.5 1.2 reshape.268
  369.7 3.5 collective-permute-done.13
  373.2 3.3 gather_fusion.6
  376.5 16.3 %fusion.18 = f32[8,16384]{1,0:T(8,128)} fusion(f32[8,16384]{1,0:T(8,128)} %get-tuple-element.122, bf16[128,8,128,128]{3,2,1,0:T(8,128)(2,1)} %param.15, bf16[128,8,8,128]{3,2,1,0:T(8,128)(2,1)S(1)} %bitcast.220, bf16[128,8]{1,0:T(8,128)(2,1)S(1)} %copy.27, f32[8,16384]{1,0:T(8,128)} %reshape.268, f32[8,16384]{1,0:T(8,128)} %copy-done.3, ...), kind=kOutput, calls=%fused_computation.33 | convolution fusion | flops 271843328 | bytes 40634400 | tf_op jit(solution)/shard_map/crtj,rtij->cri/dot_general | solution.py:60
  (100 shorter events, 5.9 us)
Async XLA Ops:
  7.2 27.7 %copy-start.20 = (s32[4096]{0:T(1024)S(1)}, s32[4096]{0:T(1024)}, u32[]{:S(2)}) copy-start(s32[4096]{0:T(1024)} %param.13) | copy-start | bytes 49156
  7.2 145.7 %reduce-scatter.2.cloned.1.call-start = ((), (), s32[]{:S(2)}) async-start(), calls=%async_computation.1 | async-start | bytes 8650752 | tf_op jit(solution)/shard_map/reduce_scatter | solution.py:112
  61.0 0.7 copy-start.22
  61.0 0.9 copy-start.21
  62.3 14.6 %copy-start.19 = (f32[16384]{0:T(1024)S(1)}, f32[16384]{0:T(1024)}, u32[]{:S(2)}) copy-start(f32[16384]{0:T(1024)} %param.18) | copy-start | bytes 196612
  76.9 108.4 %copy-start.7 = (f32[16384]{0:T(1024)}, f32[16384]{0:T(1024)S(1)}, u32[]{:S(2)}) copy-start(f32[16384]{0:T(1024)S(1)} %get-tuple-element.51) | copy-start | bytes 196612
  166.3 19.1 %copy-start.18 = (f32[8,2048]{1,0:T(8,128)}, f32[8,2048]{1,0:T(8,128)S(1)}, u32[]{:S(2)}) copy-start(f32[8,2048]{1,0:T(8,128)S(1)} %fusion.67) | copy-start | bytes 196612
  166.4 12.0 %collective-permute-start = (bf16[8,512]{1,0:T(8,128)(2,1)S(1)}, bf16[8,512]{1,0:T(8,128)(2,1)S(1)}, u32[]{:S(2)}, u32[]{:S(2)}) collective-permute-start(bf16[8,512]{1,0:T(8,128)(2,1)S(1)} %get-tuple-element.81), channel_id=1, source_target_pairs={{0,1},{1,2},{2,3},{3,4},{4,5},{5,6},{6,7},{7,8},{8,9},{9,10},{10,1... | collective-permute-start | bytes 24584 | tf_op jit(solution)/shard_map/ppermute | solution.py:25
  174.9 7.1 %collective-permute-start.1 = (bf16[8,512]{1,0:T(8,128)(2,1)S(1)}, bf16[8,512]{1,0:T(8,128)(2,1)S(1)}, u32[]{:S(2)}, u32[]{:S(2)}) collective-permute-start(bf16[8,512]{1,0:T(8,128)(2,1)S(1)} %get-tuple-element.82), channel_id=1, source_target_pairs={{1,0},{2,1},{3,2},{4,3},{5,4},{6,5},{7,6},{8,7},{9,8},{10,9},{11,1... | collective-permute-start | bytes 24584 | tf_op jit(solution)/shard_map/ppermute | solution.py:26
  182.0 3.4 copy-start.4
  200.6 4.5 %copy-start.8 = (bf16[8,16384]{1,0:T(8,128)(2,1)}, bf16[8,16384]{1,0:T(8,128)(2,1)S(1)}, u32[]{:S(2)}) copy-start(bf16[8,16384]{1,0:T(8,128)(2,1)S(1)} %get-tuple-element.49) | copy-start | bytes 786436
  200.6 6.9 %collective-permute-start.2 = (bf16[8,512]{1,0:T(8,128)(2,1)S(1)}, bf16[8,512]{1,0:T(8,128)(2,1)S(1)}, u32[]{:S(2)}, u32[]{:S(2)}) collective-permute-start(bf16[8,512]{1,0:T(8,128)(2,1)S(1)} %get-tuple-element.79), channel_id=1, source_target_pairs={{0,1},{1,2},{2,3},{3,4},{4,5},{5,6},{6,7},{7,8},{8,9},{9,10},{10,1... | collective-permute-start | bytes 24584 | tf_op jit(solution)/shard_map/ppermute | solution.py:25
  202.8 7.1 %collective-permute-start.3 = (bf16[8,512]{1,0:T(8,128)(2,1)S(1)}, bf16[8,512]{1,0:T(8,128)(2,1)S(1)}, u32[]{:S(2)}, u32[]{:S(2)}) collective-permute-start(bf16[8,512]{1,0:T(8,128)(2,1)S(1)} %get-tuple-element.80), channel_id=1, source_target_pairs={{1,0},{2,1},{3,2},{4,3},{5,4},{6,5},{7,6},{8,7},{9,8},{10,9},{11,1... | collective-permute-start | bytes 24584 | tf_op jit(solution)/shard_map/ppermute | solution.py:26
  205.1 4.8 %copy-start.9 = (bf16[8,16384]{1,0:T(8,128)(2,1)S(1)}, bf16[8,16384]{1,0:T(8,128)(2,1)}, u32[]{:S(2)}) copy-start(bf16[8,16384]{1,0:T(8,128)(2,1)} %copy-done.8) | copy-start | bytes 786436
  228.7 5.1 %copy-start.10 = (bf16[8,16384]{1,0:T(8,128)(2,1)}, bf16[8,16384]{1,0:T(8,128)(2,1)S(1)}, u32[]{:S(2)}) copy-start(bf16[8,16384]{1,0:T(8,128)(2,1)S(1)} %get-tuple-element.47) | copy-start | bytes 786436
  228.7 6.7 %collective-permute-start.4 = (bf16[8,512]{1,0:T(8,128)(2,1)S(1)}, bf16[8,512]{1,0:T(8,128)(2,1)S(1)}, u32[]{:S(2)}, u32[]{:S(2)}) collective-permute-start(bf16[8,512]{1,0:T(8,128)(2,1)S(1)} %get-tuple-element.77), channel_id=1, source_target_pairs={{0,1},{1,2},{2,3},{3,4},{4,5},{5,6},{6,7},{7,8},{8,9},{9,10},{10,1... | collective-permute-start | bytes 24584 | tf_op jit(solution)/shard_map/ppermute | solution.py:25
  231.9 7.1 %collective-permute-start.5 = (bf16[8,512]{1,0:T(8,128)(2,1)S(1)}, bf16[8,512]{1,0:T(8,128)(2,1)S(1)}, u32[]{:S(2)}, u32[]{:S(2)}) collective-permute-start(bf16[8,512]{1,0:T(8,128)(2,1)S(1)} %get-tuple-element.78), channel_id=1, source_target_pairs={{1,0},{2,1},{3,2},{4,3},{5,4},{6,5},{7,6},{8,7},{9,8},{10,9},{11,1... | collective-permute-start | bytes 24584 | tf_op jit(solution)/shard_map/ppermute | solution.py:26
  233.8 5.1 %copy-start.11 = (bf16[8,16384]{1,0:T(8,128)(2,1)S(1)}, bf16[8,16384]{1,0:T(8,128)(2,1)}, u32[]{:S(2)}) copy-start(bf16[8,16384]{1,0:T(8,128)(2,1)} %copy-done.10) | copy-start | bytes 786436
  239.0 7.6 %copy-start.5 = (f32[8,16384]{1,0:T(8,128)S(1)}, f32[8,16384]{1,0:T(8,128)}, u32[]{:S(2)}) copy-start(f32[8,16384]{1,0:T(8,128)} %get-tuple-element.118) | copy-start | bytes 1572868
  261.6 4.4 %copy-start.12 = (bf16[8,16384]{1,0:T(8,128)(2,1)}, bf16[8,16384]{1,0:T(8,128)(2,1)S(1)}, u32[]{:S(2)}) copy-start(bf16[8,16384]{1,0:T(8,128)(2,1)S(1)} %get-tuple-element.45) | copy-start | bytes 786436
  261.6 17.0 %copy-start = (f32[8,16384]{1,0:T(8,128)}, f32[8,16384]{1,0:T(8,128)S(1)}, u32[]{:S(2)}) copy-start(f32[8,16384]{1,0:T(8,128)S(1)} %get-tuple-element.46) | copy-start | bytes 1572868
  261.6 6.7 %collective-permute-start.6 = (bf16[8,512]{1,0:T(8,128)(2,1)S(1)}, bf16[8,512]{1,0:T(8,128)(2,1)S(1)}, u32[]{:S(2)}, u32[]{:S(2)}) collective-permute-start(bf16[8,512]{1,0:T(8,128)(2,1)S(1)} %get-tuple-element.75), channel_id=1, source_target_pairs={{0,1},{1,2},{2,3},{3,4},{4,5},{5,6},{6,7},{7,8},{8,9},{9,10},{10,1... | collective-permute-start | bytes 24584 | tf_op jit(solution)/shard_map/ppermute | solution.py:25
  263.9 7.1 %collective-permute-start.7 = (bf16[8,512]{1,0:T(8,128)(2,1)S(1)}, bf16[8,512]{1,0:T(8,128)(2,1)S(1)}, u32[]{:S(2)}, u32[]{:S(2)}) collective-permute-start(bf16[8,512]{1,0:T(8,128)(2,1)S(1)} %get-tuple-element.76), channel_id=1, source_target_pairs={{1,0},{2,1},{3,2},{4,3},{5,4},{6,5},{7,6},{8,7},{9,8},{10,9},{11,1... | collective-permute-start | bytes 24584 | tf_op jit(solution)/shard_map/ppermute | solution.py:26
  266.0 5.0 %copy-start.13 = (bf16[8,16384]{1,0:T(8,128)(2,1)S(1)}, bf16[8,16384]{1,0:T(8,128)(2,1)}, u32[]{:S(2)}) copy-start(bf16[8,16384]{1,0:T(8,128)(2,1)} %copy-done.12) | copy-start | bytes 786436
  293.6 5.2 %copy-start.14 = (bf16[8,16384]{1,0:T(8,128)(2,1)}, bf16[8,16384]{1,0:T(8,128)(2,1)S(1)}, u32[]{:S(2)}) copy-start(bf16[8,16384]{1,0:T(8,128)(2,1)S(1)} %get-tuple-element.43) | copy-start | bytes 786436
  293.6 17.7 %copy-start.1 = (f32[8,16384]{1,0:T(8,128)}, f32[8,16384]{1,0:T(8,128)S(1)}, u32[]{:S(2)}) copy-start(f32[8,16384]{1,0:T(8,128)S(1)} %get-tuple-element.44) | copy-start | bytes 1572868
  293.6 7.5 %collective-permute-start.8 = (bf16[8,512]{1,0:T(8,128)(2,1)S(1)}, bf16[8,512]{1,0:T(8,128)(2,1)S(1)}, u32[]{:S(2)}, u32[]{:S(2)}) collective-permute-start(bf16[8,512]{1,0:T(8,128)(2,1)S(1)} %get-tuple-element.73), channel_id=1, source_target_pairs={{0,1},{1,2},{2,3},{3,4},{4,5},{5,6},{6,7},{7,8},{8,9},{9,10},{10,1... | collective-permute-start | bytes 24584 | tf_op jit(solution)/shard_map/ppermute | solution.py:25
  296.7 7.1 %collective-permute-start.9 = (bf16[8,512]{1,0:T(8,128)(2,1)S(1)}, bf16[8,512]{1,0:T(8,128)(2,1)S(1)}, u32[]{:S(2)}, u32[]{:S(2)}) collective-permute-start(bf16[8,512]{1,0:T(8,128)(2,1)S(1)} %get-tuple-element.74), channel_id=1, source_target_pairs={{1,0},{2,1},{3,2},{4,3},{5,4},{6,5},{7,6},{8,7},{9,8},{10,9},{11,1... | collective-permute-start | bytes 24584 | tf_op jit(solution)/shard_map/ppermute | solution.py:26
  298.8 4.9 %copy-start.15 = (bf16[8,16384]{1,0:T(8,128)(2,1)S(1)}, bf16[8,16384]{1,0:T(8,128)(2,1)}, u32[]{:S(2)}) copy-start(bf16[8,16384]{1,0:T(8,128)(2,1)} %copy-done.14) | copy-start | bytes 786436
  327.2 7.6 %copy-start.16 = (bf16[8,16384]{1,0:T(8,128)(2,1)}, bf16[8,16384]{1,0:T(8,128)(2,1)S(1)}, u32[]{:S(2)}) copy-start(bf16[8,16384]{1,0:T(8,128)(2,1)S(1)} %get-tuple-element.41) | copy-start | bytes 786436
  327.2 18.9 %copy-start.2 = (f32[8,16384]{1,0:T(8,128)}, f32[8,16384]{1,0:T(8,128)S(1)}, u32[]{:S(2)}) copy-start(f32[8,16384]{1,0:T(8,128)S(1)} %get-tuple-element.42) | copy-start | bytes 1572868
  327.2 7.5 %collective-permute-start.10 = (bf16[8,512]{1,0:T(8,128)(2,1)S(1)}, bf16[8,512]{1,0:T(8,128)(2,1)S(1)}, u32[]{:S(2)}, u32[]{:S(2)}) collective-permute-start(bf16[8,512]{1,0:T(8,128)(2,1)S(1)} %get-tuple-element.71), channel_id=1, source_target_pairs={{0,1},{1,2},{2,3},{3,4},{4,5},{5,6},{6,7},{7,8},{8,9},{9,10},{10,1... | collective-permute-start | bytes 24584 | tf_op jit(solution)/shard_map/ppermute | solution.py:25
  330.4 7.1 %collective-permute-start.11 = (bf16[8,512]{1,0:T(8,128)(2,1)S(1)}, bf16[8,512]{1,0:T(8,128)(2,1)S(1)}, u32[]{:S(2)}, u32[]{:S(2)}) collective-permute-start(bf16[8,512]{1,0:T(8,128)(2,1)S(1)} %get-tuple-element.72), channel_id=1, source_target_pairs={{1,0},{2,1},{3,2},{4,3},{5,4},{6,5},{7,6},{8,7},{9,8},{10,9},{11,1... | collective-permute-start | bytes 24584 | tf_op jit(solution)/shard_map/ppermute | solution.py:26
  338.5 7.6 %copy-start.6 = (f32[8,16384]{1,0:T(8,128)S(1)}, f32[8,16384]{1,0:T(8,128)}, u32[]{:S(2)}) copy-start(f32[8,16384]{1,0:T(8,128)} %get-tuple-element.121) | copy-start | bytes 1572868
  362.0 7.7 %copy-start.3 = (f32[8,16384]{1,0:T(8,128)}, f32[8,16384]{1,0:T(8,128)S(1)}, u32[]{:S(2)}) copy-start(f32[8,16384]{1,0:T(8,128)S(1)} %get-tuple-element.40) | copy-start | bytes 1572868
  362.0 1.1 copy-start.17
  363.1 6.6 %collective-permute-start.12 = (bf16[8,512]{1,0:T(8,128)(2,1)S(1)}, bf16[8,512]{1,0:T(8,128)(2,1)S(1)}, u32[]{:S(2)}, u32[]{:S(2)}) collective-permute-start(bf16[8,512]{1,0:T(8,128)(2,1)S(1)} %get-tuple-element.69), channel_id=1, source_target_pairs={{0,1},{1,2},{2,3},{3,4},{4,5},{5,6},{6,7},{7,8},{8,9},{9,10},{10,1... | collective-permute-start | bytes 24584 | tf_op jit(solution)/shard_map/ppermute | solution.py:25
  366.1 7.1 %collective-permute-start.13 = (bf16[8,512]{1,0:T(8,128)(2,1)S(1)}, bf16[8,512]{1,0:T(8,128)(2,1)S(1)}, u32[]{:S(2)}, u32[]{:S(2)}) collective-permute-start(bf16[8,512]{1,0:T(8,128)(2,1)S(1)} %get-tuple-element.70), channel_id=1, source_target_pairs={{1,0},{2,1},{3,2},{4,3},{5,4},{6,5},{7,6},{8,7},{9,8},{10,9},{11,1... | collective-permute-start | bytes 24584 | tf_op jit(solution)/shard_map/ppermute | solution.py:26
Sparse Core Ops, SparseCore 0:
  61.1 91.7 reduce-scatter.1
where the time goes:
time: 401 us; the launch traced here: 400 us
  matrix products  124 us (31%)
  waiting for transfers between devices  96.9 us (24%)
  other arithmetic  56.6 us (14%)
  local copies, waits for them, and re-layouts  55.1 us (14%)
  starting transfers between devices  39.6 us (10%)
  between operations  14.7 us (4%)
  blocking collectives  12.4 us (3%)
    dot_general x7, matrix products, couple(): jnp.einsum('crtj,rtij->cri', picked, tiles, preferred_element_type=jnp.fl...  109 us
    reduce_scatter x1, waiting for transfers between devices, local(): lax.psum_scatter(dense_sums, 'space', scatter_dimension=1, tiled=True)  75.9 us
    gather x7, local copies, waits for them, and re-layouts, couple(): picked = blocks[:, columns] * mask_bf[None, :, :, None]  40.3 us
    scatter-add x1, other arithmetic, local(): dense_sums = jnp.zeros((thermal_states, spatial_extent * BOUNDARY_PER_CPU...  26.1 us
    ppermute x7, starting transfers between devices, extended_2(): before = lax.ppermute(last, axis, up)  25.3 us
    ppermute x7, waiting for transfers between devices, extended_2(): after = lax.ppermute(first, axis, down)  20.9 us
    convert_element_type x1, other arithmetic, local(): weight.astype(jnp.float32)[None, :]  16.5 us
    dot_general x1, matrix products, local(): jnp.einsum('rtij,rtj->ri', tile_values, spread, preferred_element_type=jn...  14.6 us
  transfers between devices with their start and end apart: 15, of which 8 were waited for; matrix products, arithmetic and copies ran while one was open for 7% of the time, Pallas kernels for 0%

commit v1 on v0

v1 whole, which is shorter than its diff:
```python
import math

import jax
import jax.numpy as jnp
import numpy as np
from jax import lax
from jax.experimental import pallas as pl
from jax.experimental.pallas import tpu as pltpu
from jax.sharding import PartitionSpec as P

SUB = 512
TILE = 128
SLOTS = 8
HALO = 4
SWEEPS = 8
COMPS = 8
LEVELS = 32

LOW_EDGE = 0.05
HIGH_EDGE = 2.0
FREQUENCY_SPACING = 0.003

STEPS = SWEEPS - 1
SURF_TILES = 16
HEAD = SURF_TILES + HALO * STEPS
TAIL = HALO * STEPS
LEND = 12
PACK = 48

F32 = jnp.float32
BF16 = jnp.bfloat16


def fourier_table():
    row = np.arange(LEVELS)
    p = (row // 2).astype(np.float64)[:, None]
    n = np.arange(LEVELS, dtype=np.float64)[None, :]
    angle = 2.0 * math.pi / LEVELS * p * n
    even = np.where(p == 0, 1.0 / LEVELS, 2.0 / LEVELS * np.cos(angle))
    odd = np.where(p == 0, np.cos(math.pi * n) / LEVELS, -2.0 / LEVELS * np.sin(angle))
    return np.where((row % 2 == 1)[:, None], odd, even).astype(np.float32)


def chebyshev_scalars():
    centre = 0.5 * (HIGH_EDGE + LOW_EDGE)
    half = 0.5 * (HIGH_EDGE - LOW_EDGE)
    stretch = centre / half
    previous = 1.0 / stretch
    scalars = []
    for _ in range(STEPS):
        current = 1.0 / (2.0 * stretch - previous)
        scalars.append((current * previous, 2.0 * current / half))
        previous = current
    return centre, scalars


def pack_kernel(counts, power, scales, nodes, out):
    targets = out.shape[0]
    row = lax.broadcasted_iota(jnp.int32, (16, TILE), 0)
    lane = lax.broadcasted_iota(jnp.int32, (16, TILE), 1)
    for d in range(targets):
        out[d, :LEVELS, :] = power[:, d * TILE : (d + 1) * TILE]
        scale = jnp.broadcast_to(scales[d : d + 1, :], (16, TILE))
        node = jnp.broadcast_to(nodes[d : d + 1, :], (16, TILE))
        weight = jnp.where(lane < counts[d], scale, 0.0)
        high = (node >> 5).astype(F32)
        low = (node & 31).astype(F32)
        aux = jnp.where(row == 0, weight, jnp.where(row == 1, high, low))
        out[d, LEVELS:, :] = aux.astype(BF16)


def scatter_kernel(table, got, out):
    sources = got.shape[0]
    place = lax.broadcasted_iota(jnp.int32, (SUB, TILE), 0).astype(F32)

    def spread(s):
        aux = got[s, LEVELS:, :].astype(F32)
        node = aux[1:2, :] * 32.0 + aux[2:3, :]
        weight = jnp.broadcast_to(aux[0:1, :], (SUB, TILE))
        hit = jnp.broadcast_to(node, (SUB, TILE)) == place
        return jnp.where(hit, weight, 0.0).astype(BF16)

    def body(i, total):
        a, b = 2 * i, 2 * i + 1
        left = jnp.concatenate([got[a, :LEVELS, :], got[b, :LEVELS, :]], axis=1)
        right = jnp.concatenate([spread(a), spread(b)], axis=1)
        return total + lax.dot_general(
            left, right, (((1,), (1,)), ((), ())), preferred_element_type=F32
        )

    sums = lax.fori_loop(0, sources // 2, body, jnp.zeros((LEVELS, SUB), F32))
    surface = jnp.dot(
        table[...], sums, precision=lax.Precision.HIGHEST, preferred_element_type=F32
    )
    for f in range(out.shape[0]):
        out[f] = surface[f * COMPS : (f + 1) * COMPS, :]


def rotated(v):
    even = lax.broadcasted_iota(jnp.int32, v.shape, 0) % 2 == 0
    return jnp.where(even, -pltpu.roll(v, COMPS - 1, 0), pltpu.roll(v, 1, 0))


def strengths(group):
    comp = lax.broadcasted_iota(jnp.int32, (COMPS, TILE), 0) + group * COMPS
    return FREQUENCY_SPACING * (comp // 2).astype(F32)


def row_product(table, tiles, vector, i):
    total = None
    for t in range(0, SLOTS, 2):
        left = jnp.concatenate([vector[table[i, t]], vector[table[i, t + 1]]], axis=1)
        right = jnp.concatenate([tiles[i, t], tiles[i, t + 1]], axis=1)
        part = lax.dot_general(
            left, right, (((1,), (1,)), ((), ())), preferred_element_type=F32
        )
        total = part if total is None else total + part
    return total


def with_ones(v):
    return jnp.concatenate([v, jnp.ones((COMPS, TILE), F32)], axis=0).astype(BF16)


def clear(vectors, count):
    blank = with_ones(jnp.zeros((COMPS, TILE), F32))

    def body(i, carry):
        vectors[0, i] = blank
        vectors[1, i] = blank
        return carry

    lax.fori_loop(0, count, body, 0)
    nothing = jnp.zeros((2 * COMPS, TILE), BF16)
    vectors[0, count] = nothing
    vectors[1, count] = nothing


def sweep_rows(first, last, table, tiles, vectors, old, film, heat, strength, direction,
               residual, total, offset, scalars):
    keep, gain = scalars

    def one(i):
        product = row_product(table, tiles, vectors.at[old], i)
        diag = product[COMPS:, :] + film[pl.ds(i, 1), :]
        v = direction[i]
        mv = diag * v - product[:COMPS, :] + strength * heat[pl.ds(i, 1), :] * rotated(v)
        r = residual[i] - mv
        new = keep * v + gain * r / diag
        return r, new

    def body(q, carry):
        base = q * HALO
        results = [one(base + j) for j in range(HALO)]
        for j, (r, new) in enumerate(results):
            i = base + j
            residual[i] = r
            direction[i] = new
            vectors[1 - old, i + offset] = with_ones(new)
            total[i] = total[i] + new
        return carry

    lax.fori_loop(first // HALO, last // HALO, body, 0)


def head_kernel(table, group, surface, film, heat, tiles_hbm, lent_hbm, surface_out, head_out,
                edge_out, tiles, vectors, direction, residual, total, edges, sems):
    chunks = (LEND + HEAD) // HALO
    lent_chunks = LEND // HALO

    def copy(q):
        rows = pl.ds(q * HALO, HALO)
        if q < lent_chunks:
            source = lent_hbm.at[rows]
        else:
            source = tiles_hbm.at[pl.ds((q - lent_chunks) * HALO, HALO)]
        return pltpu.make_async_copy(source, tiles.at[rows], sems.at[q])

    surf_chunks = SURF_TILES // HALO
    order = [lent_chunks + q for q in range(surf_chunks)]
    for k in range(1, STEPS + 1):
        order.append(lent_chunks + surf_chunks + k - 1)
        if k <= lent_chunks:
            order.append(lent_chunks - k)
    assert sorted(order) == list(range(chunks))
    for q in order:
        copy(q).start()

    centre, scalars = chebyshev_scalars()
    strength = strengths(group[0])
    clear(vectors, LEND + HEAD + 2 * HALO)
    zero = jnp.zeros((COMPS, TILE), F32)

    def blank(i, carry):
        direction[i] = zero
        residual[i] = zero
        total[i] = zero
        return carry

    lax.fori_loop(0, LEND + HEAD, blank, 0)

    for j in range(SURF_TILES):
        part = surface[j // HALO, :, (j % HALO) * TILE : (j % HALO + 1) * TILE]
        surface_out[:, j * TILE : (j + 1) * TILE] = part
        residual[LEND + j] = part

    for q in range(surf_chunks):
        copy(lent_chunks + q).wait()

    def start(q, carry):
        base = LEND + q * HALO
        products = [row_product(table, tiles, vectors.at[1], base + j) for j in range(HALO)]
        for j, product in enumerate(products):
            i = base + j
            diag = product[COMPS:, :] + film[pl.ds(i, 1), :]
            new = residual[i] / (centre * diag)
            direction[i] = new
            total[i] = new
            vectors[0, i + HALO] = with_ones(new)
        return carry

    lax.fori_loop(0, surf_chunks, start, 0)
    for j in range(HALO):
        edges[0, j] = direction[LEND + j]

    for k in range(1, STEPS + 1):
        copy(lent_chunks + surf_chunks + k - 1).wait()
        if k <= lent_chunks:
            copy(lent_chunks - k).wait()
        low = LEND - HALO * min(k, STEPS - k)
        high = LEND + SURF_TILES + HALO * k
        sweep_rows(low, high, table, tiles, vectors, (k - 1) % 2, film, heat, strength, direction,
                   residual, total, HALO, scalars[k - 1])
        for j in range(HALO):
            edges[k, j] = direction[LEND + j]

    for j in range(HEAD):
        head_out[:, j * TILE : (j + 1) * TILE] = total[LEND + j]
    for p in range(SWEEPS // 2):
        for j in range(HALO):
            edge_out[p, j] = jnp.concatenate([edges[2 * p, j], edges[2 * p + 1, j]], axis=0).astype(BF16)


def tail_kernel(table, group, edge, film, heat, head, tiles_hbm, out, tiles, vectors, direction,
                residual, total, sems):
    row_tiles = out.shape[1] // TILE
    first = row_tiles - TAIL
    chunks = TAIL // HALO

    def copy(q):
        rows = pl.ds(q * HALO, HALO)
        source = tiles_hbm.at[pl.ds(first + q * HALO, HALO)]
        return pltpu.make_async_copy(source, tiles.at[rows], sems.at[q])

    for q in reversed(range(chunks)):
        copy(q).start()

    _, scalars = chebyshev_scalars()
    strength = strengths(group[0])
    clear(vectors, TAIL + 2 * HALO)
    zero = jnp.zeros((COMPS, TILE), F32)

    def blank(i, carry):
        direction[i] = zero
        residual[i] = zero
        total[i] = zero
        return carry

    lax.fori_loop(0, TAIL, blank, 0)
    out[:, : HEAD * TILE] = head[...]
    out[:, HEAD * TILE : first * TILE] = jnp.zeros((COMPS, (first - HEAD) * TILE), F32)

    for k in range(1, STEPS + 1):
        old = (k - 1) % 2
        for j in range(HALO):
            pair = edge[(k - 1) // 2, j].astype(F32)
            vectors[old, HALO + TAIL + j] = with_ones(pair[old * COMPS : (old + 1) * COMPS, :])
        copy(chunks - k).wait()
        sweep_rows(TAIL - HALO * k, TAIL, table, tiles, vectors, old, film, heat, strength,
                   direction, residual, total, HALO, scalars[k - 1])

    for j in range(TAIL):
        out[:, (first + j) * TILE : (first + j + 1) * TILE] = total[j]


def vmem():
    return pl.BlockSpec(memory_space=pltpu.VMEM)


def smem():
    return pl.BlockSpec(memory_space=pltpu.SMEM)


def hbm():
    return pl.BlockSpec(memory_space=pl.ANY)


def local(
    boundary_power_density,
    face_scales,
    face_node,
    send_counts,
    tile_values,
    tile_mask,
    tile_columns,
    film_sink,
    capacity,
):
    parts = lax.axis_size("space")
    groups = lax.axis_size("freq")
    place = lax.axis_index("space")
    group = lax.axis_index("freq").astype(jnp.int32).reshape(1)
    nodes_here = film_sink.shape[0]
    row_tiles = nodes_here // TILE
    up = [(i, i + 1) for i in range(parts - 1)]
    down = [(i + 1, i) for i in range(parts - 1)]

    film = film_sink.reshape(row_tiles, TILE)
    heat = capacity.reshape(row_tiles, TILE)

    lent = lax.ppermute(lax.slice_in_dim(tile_values, row_tiles - LEND, row_tiles), "space", up)
    places = jnp.where(tile_mask > 0, tile_columns, -1).astype(F32)
    facts = jnp.concatenate(
        [
            film[row_tiles - LEND :],
            heat[row_tiles - LEND :],
            jnp.pad(places[row_tiles - LEND :], ((0, 0), (0, TILE - SLOTS))),
        ],
        axis=0,
    )
    facts = lax.ppermute(facts, "space", up)
    lent_film = jnp.where(place == 0, 1.0, facts[:LEND])
    lent_places = facts[2 * LEND :, :SLOTS].astype(jnp.int32)
    blank = LEND + HEAD + 2 * HALO
    own = jnp.where(tile_mask > 0, tile_columns, -1)
    lent_table = jnp.where(
        (lent_places < 0) | (place == 0), blank, lent_places - (row_tiles - LEND)
    )
    head_own = own[:HEAD]
    head_table = jnp.concatenate(
        [lent_table, jnp.where(head_own < 0, blank, head_own + LEND)], axis=0
    )
    tail_own = own[row_tiles - TAIL :]
    tail_table = jnp.where(tail_own < 0, TAIL + 2 * HALO, tail_own - (row_tiles - TAIL))
    head_film = jnp.concatenate([lent_film, film[:HEAD]], axis=0)
    head_heat = jnp.concatenate([facts[LEND : 2 * LEND], heat[:HEAD]], axis=0)

    packed = pl.pallas_call(
        pack_kernel,
        out_shape=jax.ShapeDtypeStruct((parts, PACK, TILE), BF16),
        in_specs=[smem(), vmem(), vmem(), vmem()],
        out_specs=vmem(),
    )(
        send_counts,
        boundary_power_density,
        face_scales.reshape(parts, TILE).astype(F32),
        face_node.reshape(parts, TILE),
    )
    got = lax.all_to_all(packed, "space", 0, 0)
    mixed = pl.pallas_call(
        scatter_kernel,
        out_shape=jax.ShapeDtypeStruct((groups, COMPS, SUB), F32),
        in_specs=[vmem(), vmem()],
        out_specs=vmem(),
    )(jnp.asarray(fourier_table()), got)
    mixed = lax.all_to_all(mixed, "freq", 0, 0)

    rows = LEND + HEAD
    surface, head, edge = pl.pallas_call(
        head_kernel,
        out_shape=(
            jax.ShapeDtypeStruct((COMPS, SURF_TILES * TILE), F32),
            jax.ShapeDtypeStruct((COMPS, HEAD * TILE), F32),
            jax.ShapeDtypeStruct((SWEEPS // 2, HALO, 2 * COMPS, TILE), BF16),
        ),
        in_specs=[smem(), smem(), vmem(), vmem(), vmem(), hbm(), hbm()],
        out_specs=(vmem(), vmem(), vmem()),
        scratch_shapes=[
            pltpu.VMEM((rows, SLOTS, TILE, TILE), BF16),
            pltpu.VMEM((2, rows + 2 * HALO + 1, 2 * COMPS, TILE), BF16),
            pltpu.VMEM((rows, COMPS, TILE), F32),
            pltpu.VMEM((rows, COMPS, TILE), F32),
            pltpu.VMEM((rows, COMPS, TILE), F32),
            pltpu.VMEM((SWEEPS, HALO, COMPS, TILE), F32),
            pltpu.SemaphoreType.DMA((rows // HALO,)),
        ],
        compiler_params=pltpu.CompilerParams(vmem_limit_bytes=40 << 20),
    )(head_table, group, mixed, head_film, head_heat, tile_values, lent)

    edge = lax.ppermute(edge, "space", down)

    temperature = pl.pallas_call(
        tail_kernel,
        out_shape=jax.ShapeDtypeStruct((COMPS, nodes_here), F32),
        in_specs=[smem(), smem(), vmem(), vmem(), vmem(), vmem(), hbm()],
        out_specs=vmem(),
        scratch_shapes=[
            pltpu.VMEM((TAIL, SLOTS, TILE, TILE), BF16),
            pltpu.VMEM((2, TAIL + 2 * HALO + 1, 2 * COMPS, TILE), BF16),
            pltpu.VMEM((TAIL, COMPS, TILE), F32),
            pltpu.VMEM((TAIL, COMPS, TILE), F32),
            pltpu.VMEM((TAIL, COMPS, TILE), F32),
            pltpu.SemaphoreType.DMA((TAIL // HALO,)),
        ],
        compiler_params=pltpu.CompilerParams(vmem_limit_bytes=40 << 20),
    )(
        tail_table,
        group,
        edge,
        film[row_tiles - TAIL :],
        heat[row_tiles - TAIL :],
        head,
        tile_values,
    )
    return surface, temperature


def solution(mesh):
    placed = (
        P(None, ("freq", "space")),
        P(("freq", "space")),
        P(("freq", "space")),
        P(("freq", "space")),
        P("space", None, None, None),
        P("space", None),
        P("space", None),
        P("space"),
        P("space"),
    )
    return jax.shard_map(
        local,
        mesh=mesh,
        in_specs=placed,
        out_specs=(P("freq", "space"), P("freq", "space")),
        check_vma=False,
    )
```

time: 401 us -> 120 us (0.30)
  matrix products: 124 us -> 0 us
  waiting for transfers between devices: 96.9 us -> 38.4 us
  other arithmetic: 56.6 us -> 0.69 us
  Pallas kernels: 0 us -> 53.6 us
  local copies, waits for them, and re-layouts: 55.1 us -> 4.28 us
  starting transfers between devices: 39.6 us -> 20.3 us
  between operations: 14.7 us -> 0.84 us
  blocking collectives: 12.4 us -> 0 us
    dot_general x9 -> x0, matrix products: 124 us -> none  [the longest x7 109 us: couple(): jnp.einsum('crtj,rtij->cri', picked, tiles, preferred_element_type=jnp.fl...]
    reduce_scatter x1 -> x0, waiting for transfers between devices: 75.9 us -> none  [local(): lax.psum_scatter(dense_sums, 'space', scatter_dimension=1, tiled=True)]
    pallas_call x0 -> x4, Pallas kernels: none -> 53.6 us  [the longest x1 32.7 us: local(): pl.pallas_call(head_kernel, out_shape=(jax.ShapeDtypeStruct((COMPS, SURF_...]
    gather x9 -> x0, local copies, waits for them, and re-layouts: 44.2 us -> none  [the longest x7 40.3 us: couple(): picked = blocks[:, columns] * mask_bf[None, :, :, None]]
    ppermute x14 -> x3, starting transfers between devices: 39.6 us -> 7.46 us  [the longest x1 3.24 us: local(): edge = lax.ppermute(edge, 'space', down)]
    scatter-add x1 -> x0, other arithmetic: 26.1 us -> none  [local(): dense_sums = jnp.zeros((thermal_states, spatial_extent * BOUNDARY_PER_CPU...]
    convert_element_type x3 -> x2, other arithmetic: 16.5 us -> 0.61 us  [the longest x1 0.61 us: local(): face_scales.reshape(parts, TILE).astype(F32)]
    all_to_all x0 -> x2, starting transfers between devices: none -> 12.8 us  [the longest x1 8.65 us: local(): got = lax.all_to_all(packed, 'space', 0, 0)]
  transfers between devices with their start and end apart: 15 -> 5, of which waited for: 8 -> 4; matrix products, arithmetic and copies ran while one was open for 7% -> 1% of each run, Pallas kernels for 0% -> 6%
where the time goes in v1:
time: 120 us; the launch traced here: 118 us
  Pallas kernels  53.6 us (45%)
  waiting for transfers between devices  38.4 us (32%)
  starting transfers between devices  20.3 us (17%)
  local copies, waits for them, and re-layouts  4.28 us (4%)
    pallas_call x1, Pallas kernels, local(): pl.pallas_call(head_kernel, out_shape=(jax.ShapeDtypeStruct((COMPS, SURF_...  32.7 us
    ppermute x1, waiting for transfers between devices, local(): facts = lax.ppermute(facts, 'space', up)  24.6 us
    pallas_call x1, Pallas kernels, local(): pl.pallas_call(tail_kernel, out_shape=jax.ShapeDtypeStruct((COMPS, nodes_...  14.1 us
    all_to_all x1, starting transfers between devices, local(): got = lax.all_to_all(packed, 'space', 0, 0)  8.65 us
    pallas_call x1, Pallas kernels, local(): pl.pallas_call(scatter_kernel, out_shape=jax.ShapeDtypeStruct((groups, CO...  5.04 us
    all_to_all x1, waiting for transfers between devices, local(): got = lax.all_to_all(packed, 'space', 0, 0)  4.93 us
    all_to_all x1, waiting for transfers between devices, local(): mixed = lax.all_to_all(mixed, 'freq', 0, 0)  4.47 us
    ppermute x1, waiting for transfers between devices, local(): edge = lax.ppermute(edge, 'space', down)  4.43 us
  transfers between devices with their start and end apart: 5, of which 4 were waited for; matrix products, arithmetic and copies ran while one was open for 1% of the time, Pallas kernels for 6%

profile of v1, /device:TPU:97, one launch (start us, length us, event | category | flops | bytes accessed | tf_op | source)
XLA Modules:
  0.0 118.1 jit_solution(216075047328336172)
XLA Ops:
  0.6 0.0 copy-start.3
  0.6 0.0 copy-start.4
  0.7 0.0 copy-start
  0.7 0.0 copy-start.1
  0.7 0.0 copy-start.2
  0.7 4.0 %slice.118 = bf16[12,8,128,128]{3,2,1,0:T(8,128)(2,1)} slice(bf16[128,8,128,128]{3,2,1,0:T(8,128)(2,1)} %tiles_hbm.3), slice={[116:128], [0:8], [0:128], [0:128]} | slice | bytes 6291456 | tf_op jit(solution)/shard_map/slice | solution.py:321
  4.7 2.3 %collective-permute-start.1 = (bf16[12,8,128,128]{3,2,1,0:T(8,128)(2,1)}, bf16[12,8,128,128]{3,2,1,0:T(8,128)(2,1)S(1)}, u32[]{:S(2)}, u32[]{:S(2)}) collective-permute-start(bf16[12,8,128,128]{3,2,1,0:T(8,128)(2,1)} %slice.118), channel_id=1, source_target_pairs={{0,1},{1,2},{2,3},{3,4},{4,5},{5,6},{6,7},{7,8},{8,9},{9,10},{10,1... | collective-permute-start | bytes 9437192 | tf_op jit(solution)/shard_map/ppermute | solution.py:321
  7.0 0.0 copy-done.3
  7.0 0.1 copy.25
  7.1 0.0 copy-done.4
  7.1 0.1 copy.24
  7.3 0.0 copy-done
  7.3 0.0 copy-done.1
  7.3 1.9 %collective-permute-start = (f32[36,128]{1,0:T(8,128)S(1)}, f32[36,128]{1,0:T(8,128)S(1)}, u32[]{:S(2)}, u32[]{:S(2)}) collective-permute-start(f32[36,128]{1,0:T(8,128)S(1)} %select_maximum_fusion), channel_id=1, source_target_pairs={{0,1},{1,2},{2,3},{3,4},{4,5},{5,6},{6,7},{7,8},{8,9},{9,10},{10,1... | collective-permute-start | bytes 55304 | tf_op jit(solution)/shard_map/ppermute | solution.py:331
  9.3 0.0 copy-done.2
  9.3 0.6 bitcast_convert_fusion.scales
  9.9 1.8 %shard_map.113 = bf16[32,48,128]{2,1,0:T(8,128)(2,1)} custom-call(s32[32]{0:T(128)} %counts.1, bf16[32,4096]{1,0:T(8,128)(2,1)} %power.1, f32[32,128]{1,0:T(8,128)} %bitcast_convert_fusion.scales, s32[32,128]{1,0:T(8,128)} %bitcast.17), custom_call_target="tpu_custom_call" | custom-call | tf_op jit(solution)/shard_map/pallas_call | solution.py:348
  11.7 8.6 %all-to-all-start = ((bf16[32,48,128]{2,1,0:T(8,128)(2,1)}), bf16[32,48,128]{2,1,0:T(8,128)(2,1)}, u32[]{:S(2)}, u32[]{:S(2)}) async-start(bf16[32,48,128]{2,1,0:T(8,128)(2,1)} %shard_map.113), calls=%async_computation | async-start | bytes 786432 | tf_op jit(solution)/shard_map/all_to_all | solution.py:359
  20.4 24.6 %collective-permute-done = f32[36,128]{1,0:T(8,128)S(1)} collective-permute-done((f32[36,128]{1,0:T(8,128)S(1)}, f32[36,128]{1,0:T(8,128)S(1)}, u32[]{:S(2)}, u32[]{:S(2)}) %collective-permute-start) | collective-permute-done | bytes 18464 | tf_op jit(solution)/shard_map/ppermute | solution.py:331
  45.0 4.9 %all-to-all-done.got = bf16[32,48,128]{2,1,0:T(8,128)(2,1)} async-done(((bf16[32,48,128]{2,1,0:T(8,128)(2,1)}), bf16[32,48,128]{2,1,0:T(8,128)(2,1)}, u32[]{:S(2)}, u32[]{:S(2)}) %all-to-all-start) | async-done | bytes 393248 | tf_op jit(solution)/shard_map/all_to_all | solution.py:359
  49.9 5.0 %shard_map.114 = f32[4,8,512]{2,1,0:T(8,128)} custom-call(f32[32,32]{1,0:T(8,128)} %constant.35.clone.table, bf16[32,48,128]{2,1,0:T(8,128)(2,1)} %all-to-all-done.got), custom_call_target="tpu_custom_call" | custom-call | tf_op jit(solution)/shard_map/pallas_call | solution.py:360
  55.0 4.2 %all-to-all-start.1 = ((f32[4,8,512]{2,1,0:T(8,128)}), f32[4,8,512]{2,1,0:T(8,128)S(1)}, u32[]{:S(2)}, u32[]{:S(2)}) async-start(f32[4,8,512]{2,1,0:T(8,128)} %shard_map.114), calls=%async_computation.1 | async-start | bytes 131072 | tf_op jit(solution)/shard_map/all_to_all | solution.py:366
  59.2 4.5 %all-to-all-done.1.surface = f32[4,8,512]{2,1,0:T(8,128)S(1)} async-done(((f32[4,8,512]{2,1,0:T(8,128)}), f32[4,8,512]{2,1,0:T(8,128)S(1)}, u32[]{:S(2)}, u32[]{:S(2)}) %all-to-all-start.1) | async-done | bytes 65568 | tf_op jit(solution)/shard_map/all_to_all | solution.py:366
  63.6 0.0 collective-permute-done.1.lent_hbm
  63.6 32.7 %shard_map.115 = (f32[8,2048]{1,0:T(8,128)}, f32[8,5632]{1,0:T(8,128)S(1)}, bf16[4,4,16,128]{3,2,1,0:T(8,128)(2,1)S(1)}) custom-call(s32[56,8]{1,0:T(8,128)S(1)} %pad_add_fusion.table, s32[1]{0:T(128)} %bitcast.2.group, f32[4,8,512]{2,1,0:T(8,128)S(1)} %all-to-all-done.1.surface, f32[56,128]{1,0:T(8,128)S(1)} %pad_maximum_fusion.film, ...), custom_call_target="tpu_custom_call" | custom-call | tf_op jit(solution)/shard_map/pallas_call | solution.py:369
  96.3 3.2 %collective-permute-start.2 = (bf16[4,4,16,128]{3,2,1,0:T(8,128)(2,1)S(1)}, bf16[4,4,16,128]{3,2,1,0:T(8,128)(2,1)S(1)}, u32[]{:S(2)}, u32[]{:S(2)}) collective-permute-start(bf16[4,4,16,128]{3,2,1,0:T(8,128)(2,1)S(1)} %get-tuple-element.6), channel_id=1, source_target_pairs={{1,0},{2,1},{3,2},{4,3},{5,4},{6,5},{7,6},{8,7},{9,8},{10,9},{11,1... | collective-permute-start | bytes 196616 | tf_op jit(solution)/shard_map/ppermute | solution.py:390
  99.6 4.4 %collective-permute-done.2.edge = bf16[4,4,16,128]{3,2,1,0:T(8,128)(2,1)S(1)} collective-permute-done((bf16[4,4,16,128]{3,2,1,0:T(8,128)(2,1)S(1)}, bf16[4,4,16,128]{3,2,1,0:T(8,128)(2,1)S(1)}, u32[]{:S(2)}, u32[]{:S(2)}) %collective-permute-start.2) | collective-permute-done | bytes 65568 | tf_op jit(solution)/shard_map/ppermute | solution.py:390
  104.0 14.1 %shard_map.116 = f32[8,16384]{1,0:T(8,128)} custom-call(s32[28,8]{1,0:T(8,128)S(1)} %add_select_fusion.1.table, s32[1]{0:T(128)} %bitcast.2.group, bf16[4,4,16,128]{3,2,1,0:T(8,128)(2,1)S(1)} %collective-permute-done.2.edge, f32[28,128]{1,0:T(8,128)S(1)} %get-tuple-element.13.film, f32[28,128]{1,0:T(8,128)S(1)} %get-tuple-element.12.heat, ...), custom_call_target="tpu_custom_call" | custom-call | tf_op jit(solution)/shard_map/pallas_call | solution.py:392
  (15 shorter events, 0.1 us)
Async XLA Ops:
  0.6 6.4 %copy-start.3 = (s32[128,8]{0,1:T(8,128)S(1)}, s32[128,8]{0,1:T(8,128)}, u32[]{:S(2)}) copy-start(s32[128,8]{0,1:T(8,128)} %param.16) | copy-start | bytes 12292
  0.6 6.5 %copy-start.4 = (s32[128,8]{0,1:T(8,128)S(1)}, s32[128,8]{0,1:T(8,128)}, u32[]{:S(2)}) copy-start(s32[128,8]{0,1:T(8,128)} %param.15) | copy-start | bytes 12292
  0.7 6.6 %copy-start = (f32[16384]{0:T(1024)S(1)}, f32[16384]{0:T(1024)}, u32[]{:S(2)}) copy-start(f32[16384]{0:T(1024)} %param.17) | copy-start | bytes 196612
  0.7 6.6 %copy-start.1 = (f32[16384]{0:T(1024)S(1)}, f32[16384]{0:T(1024)}, u32[]{:S(2)}) copy-start(f32[16384]{0:T(1024)} %param.18) | copy-start | bytes 196612
  0.7 8.6 %copy-start.2 = (bf16[4096]{0:T(1024)(128)(2,1)S(1)}, bf16[4096]{0:T(1024)(128)(2,1)}, u32[]{:S(2)}) copy-start(bf16[4096]{0:T(1024)(128)(2,1)} %param.11) | copy-start | bytes 24580
  4.7 58.9 %collective-permute-start.1 = (bf16[12,8,128,128]{3,2,1,0:T(8,128)(2,1)}, bf16[12,8,128,128]{3,2,1,0:T(8,128)(2,1)S(1)}, u32[]{:S(2)}, u32[]{:S(2)}) collective-permute-start(bf16[12,8,128,128]{3,2,1,0:T(8,128)(2,1)} %slice.118), channel_id=1, source_target_pairs={{0,1},{1,2},{2,3},{3,4},{4,5},{5,6},{6,7},{7,8},{8,9},{9,10},{10,1... | collective-permute-start | bytes 9437192 | tf_op jit(solution)/shard_map/ppermute | solution.py:321
  7.3 37.6 %collective-permute-start = (f32[36,128]{1,0:T(8,128)S(1)}, f32[36,128]{1,0:T(8,128)S(1)}, u32[]{:S(2)}, u32[]{:S(2)}) collective-permute-start(f32[36,128]{1,0:T(8,128)S(1)} %select_maximum_fusion), channel_id=1, source_target_pairs={{0,1},{1,2},{2,3},{3,4},{4,5},{5,6},{6,7},{7,8},{8,9},{9,10},{10,1... | collective-permute-start | bytes 55304 | tf_op jit(solution)/shard_map/ppermute | solution.py:331
  11.7 38.3 %all-to-all-start = ((bf16[32,48,128]{2,1,0:T(8,128)(2,1)}), bf16[32,48,128]{2,1,0:T(8,128)(2,1)}, u32[]{:S(2)}, u32[]{:S(2)}) async-start(bf16[32,48,128]{2,1,0:T(8,128)(2,1)} %shard_map.113), calls=%async_computation | async-start | bytes 786432 | tf_op jit(solution)/shard_map/all_to_all | solution.py:359
  55.0 8.7 %all-to-all-start.1 = ((f32[4,8,512]{2,1,0:T(8,128)}), f32[4,8,512]{2,1,0:T(8,128)S(1)}, u32[]{:S(2)}, u32[]{:S(2)}) async-start(f32[4,8,512]{2,1,0:T(8,128)} %shard_map.114), calls=%async_computation.1 | async-start | bytes 131072 | tf_op jit(solution)/shard_map/all_to_all | solution.py:366
  96.3 7.7 %collective-permute-start.2 = (bf16[4,4,16,128]{3,2,1,0:T(8,128)(2,1)S(1)}, bf16[4,4,16,128]{3,2,1,0:T(8,128)(2,1)S(1)}, u32[]{:S(2)}, u32[]{:S(2)}) collective-permute-start(bf16[4,4,16,128]{3,2,1,0:T(8,128)(2,1)S(1)} %get-tuple-element.6), channel_id=1, source_target_pairs={{1,0},{2,1},{3,2},{4,3},{5,4},{6,5},{7,6},{8,7},{9,8},{10,9},{11,1... | collective-permute-start | bytes 196616 | tf_op jit(solution)/shard_map/ppermute | solution.py:390

commit v2 on v0

v2 whole, which is shorter than its diff:
```python
import math

import jax
import jax.numpy as jnp
import numpy as np
from jax import lax
from jax.experimental import pallas as pl
from jax.experimental.pallas import tpu as pltpu
from jax.sharding import PartitionSpec as P

SUB = 512
TILE = 128
SLOTS = 8
HALO = 4
SWEEPS = 8
COMPS = 8
LEVELS = 32

LOW_EDGE = 0.05
HIGH_EDGE = 2.0
FREQUENCY_SPACING = 0.003

STEPS = SWEEPS - 1
SURF_TILES = 16
HEAD = SURF_TILES + HALO * STEPS
TAIL = HALO * STEPS
LEND = 12
PIECES = (12,)
PACK = 48

HEAD_ROWS = LEND + HEAD
HEAD_BLANK = HEAD_ROWS + 2 * HALO
TAIL_BLANK = TAIL + 2 * HALO

F32 = jnp.float32
BF16 = jnp.bfloat16


def fourier_table():
    row = np.arange(LEVELS)
    p = (row // 2).astype(np.float64)[:, None]
    n = np.arange(LEVELS, dtype=np.float64)[None, :]
    angle = 2.0 * math.pi / LEVELS * p * n
    even = np.where(p == 0, 1.0 / LEVELS, 2.0 / LEVELS * np.cos(angle))
    odd = np.where(p == 0, np.cos(math.pi * n) / LEVELS, -2.0 / LEVELS * np.sin(angle))
    return np.where((row % 2 == 1)[:, None], odd, even).astype(np.float32)


CENTRE = 0.5 * (HIGH_EDGE + LOW_EDGE)


def chebyshev_scalars():
    half = 0.5 * (HIGH_EDGE - LOW_EDGE)
    stretch = CENTRE / half
    previous = 1.0 / stretch
    scalars = []
    for _ in range(STEPS):
        current = 1.0 / (2.0 * stretch - previous)
        scalars.append((current * previous, 2.0 * current / half))
        previous = current
    return scalars


def needs(task, low, high):
    k, g = task
    if k == 1:
        return []
    return [(k - 1, h) for h in (g - 1, g, g + 1) if low(k - 1) <= h <= high(k - 1)]


def in_order(tasks):
    steps = sorted({k for k, _ in tasks})
    return [sorted(t for t in tasks if t[0] == k) for k in steps]


def head_plan():
    def low(k):
        return -min(k, STEPS - k)

    def high(k):
        return 3 + k

    def reads(task):
        return needs(task, lambda k: -k, high)

    every = {(k, g) for k in range(1, STEPS + 1) for g in range(low(k), high(k) + 1)}
    free = set()
    for task in sorted(every):
        if task[1] >= 0 and all(n in free for n in reads(task)):
            free.add(task)
    return in_order(free), in_order(every - free)


def tail_plan():
    return [[(k, g) for g in range(-k, 0)] for k in range(1, STEPS + 1)]


def pack_kernel(counts, power, scales, nodes, columns, mask, film, heat, out, head_table, tail_table, facts):
    targets = out.shape[0]
    row_tiles = film.shape[0]
    row = lax.broadcasted_iota(jnp.int32, (16, TILE), 0)
    lane = lax.broadcasted_iota(jnp.int32, (16, TILE), 1)
    for d in range(targets):
        out[d, :LEVELS, :] = power[:, d * TILE : (d + 1) * TILE]
        scale = jnp.broadcast_to(scales[d : d + 1, :].astype(F32), (16, TILE))
        node = jnp.broadcast_to(nodes[d : d + 1, :], (16, TILE))
        weight = jnp.where(lane < counts[d], scale, 0.0)
        high = (node >> 5).astype(F32)
        low = (node & 31).astype(F32)
        aux = jnp.where(row == 0, weight, jnp.where(row == 1, high, low))
        out[d, LEVELS:, :] = aux.astype(BF16)
    live = mask[...] > 0
    head_table[...] = jnp.where(live, columns[...] + LEND, HEAD_BLANK)
    tail_table[...] = jnp.where(live, columns[...] - (row_tiles - TAIL), TAIL_BLANK)
    lent_table = jnp.where(live, columns[...] - (row_tiles - LEND), HEAD_BLANK)
    facts[:SLOTS, :] = lent_table.astype(F32)
    facts[SLOTS : SLOTS + LEND, :] = film[row_tiles - LEND :, :]
    facts[SLOTS + LEND :, :] = heat[row_tiles - LEND :, :]


def scatter_kernel(group, table, got, *rest):
    out, (sums, surface) = rest[:-2], rest[-2:]
    sources = got.shape[0]
    span = 8
    place = lax.broadcasted_iota(jnp.int32, (SUB, TILE), 0).astype(F32)

    def spread(s):
        aux = got[s, LEVELS:, :].astype(F32)
        node = aux[1:2, :] * 32.0 + aux[2:3, :]
        weight = jnp.broadcast_to(aux[0:1, :], (SUB, TILE))
        hit = jnp.broadcast_to(node, (SUB, TILE)) == place
        return jnp.where(hit, weight, 0.0).astype(BF16)

    sums[...] = jnp.zeros((LEVELS, SUB), F32)

    def body(i, carry):
        first = i * span
        left = jnp.concatenate([got[first + n, :LEVELS, :] for n in range(span)], axis=1)
        right = jnp.concatenate([spread(first + n) for n in range(span)], axis=1)
        sums[...] += lax.dot_general(
            left, right, (((1,), (1,)), ((), ())), preferred_element_type=F32
        )
        return carry

    lax.fori_loop(0, sources // span, body, 0)
    surface[...] = jnp.dot(
        table[...], sums[...], precision=lax.Precision.HIGHEST, preferred_element_type=F32
    )
    for shift in range(len(out)):
        f = lax.rem(group[0] + shift, len(out))
        out[shift][...] = surface[pl.ds(pl.multiple_of(f * COMPS, COMPS), COMPS), :]


def with_ones(v):
    return jnp.concatenate([v, jnp.ones((COMPS, TILE), F32)], axis=0).astype(BF16)


def lend_kernel(tiles_hbm, *rest):
    pieces, sems = rest[:-1], rest[-1]
    first = tiles_hbm.shape[0] - sum(piece.shape[0] for piece in pieces)
    copies = []
    for n, piece in enumerate(pieces):
        rows = pl.ds(first, piece.shape[0])
        copies.append(pltpu.make_async_copy(tiles_hbm.at[rows], piece, sems.at[n]))
        copies[-1].start()
        first += piece.shape[0]
    for copy in copies:
        copy.wait()


def transpose_tiles(first, tiles_hbm, out_hbm, buffer, tiles, sems, out_sem):
    depth = buffer.shape[0]
    chunks = tiles.shape[0] // HALO

    def copy(q, slot):
        return pltpu.make_async_copy(
            tiles_hbm.at[pl.ds(first + q * HALO, HALO)], buffer.at[slot], sems.at[slot]
        )

    def back(q):
        rows = pl.ds(q * HALO, HALO)
        return pltpu.make_async_copy(tiles.at[rows], out_hbm.at[rows], out_sem.at[q])

    for q in range(depth):
        copy(q, q).start()

    def chunk(q, carry):
        slot = lax.rem(q, depth)
        copy(q, slot).wait()
        for j in range(HALO):
            for t in range(SLOTS):
                tiles[q * HALO + j, t] = buffer[slot, j, t].T
        back(q).start()

        @pl.when(q + depth < chunks)
        def _():
            copy(q + depth, slot).start()

        return carry

    lax.fori_loop(0, chunks, chunk, 0)
    return [back(q) for q in range(chunks)]


def prep_kernel(mask, film, tiles_hbm, out_hbm, diag, buffer, tiles, sems, out_sem):
    copies = transpose_tiles(0, tiles_hbm, out_hbm, buffer, tiles, sems, out_sem)

    def sums(i, carry):
        rowsum = jnp.zeros((COMPS, TILE), F32)
        for t in range(SLOTS):
            tile = tiles[i, t].astype(F32).reshape(TILE // COMPS, COMPS, TILE)
            rowsum += jnp.sum(tile, axis=0) * mask[t, i].astype(F32)
        diag[i] = jnp.broadcast_to(
            jnp.sum(rowsum, axis=0, keepdims=True) + film[pl.ds(i, 1), :], (COMPS, TILE)
        )
        return carry

    lax.fori_loop(0, SURF_TILES, sums, 0)
    for copy in copies:
        copy.wait()


def rotated(v):
    even = lax.broadcasted_iota(jnp.int32, v.shape, 0) % 2 == 0
    return jnp.where(even, -pltpu.roll(v, COMPS - 1, 0), pltpu.roll(v, 1, 0))


def strengths(group):
    comp = lax.broadcasted_iota(jnp.int32, (COMPS, TILE), 0) + group * COMPS
    return FREQUENCY_SPACING * (comp // 2).astype(F32)


class Rows:
    def __init__(self, groups, first, transposed, source, buffer, sems, table, film, heat, fact_row, table_row,
                 extra=0.0):
        self.transposed, self.table, self.film, self.heat = transposed, table, film, heat
        self.first, self.fact_row, self.table_row, self.extra = first, fact_row, table_row, extra
        self.buffer, self.slot, self.copies = buffer, {}, {}
        for n, g in enumerate(groups):
            rows = pl.ds(n * HALO, HALO)
            self.slot[g] = n * HALO
            self.copies[g] = pltpu.make_async_copy(source(g), buffer.at[rows], sems.at[first + n])

    def fetch(self, g):
        self.copies[g].start()

    def wait(self, g):
        copy = self.copies.pop(g, None)
        if copy is not None:
            copy.wait()

    def product(self, vector, g, j):
        i = self.slot[g] + j
        row = HALO * g + j + self.table_row
        left = jnp.concatenate([vector[self.table[t, row]] for t in range(SLOTS)], axis=1)
        right = jnp.concatenate(
            [self.buffer[i, t] for t in range(SLOTS)], axis=0 if self.transposed else 1
        )
        return lax.dot_general(
            left,
            right,
            (((1,), (0 if self.transposed else 1,)), ((), ())),
            preferred_element_type=F32,
        )

    def diagonal(self, product, g, j):
        row = HALO * g + j + self.fact_row
        return product[COMPS:, :] + (self.film[row : row + 1, :] + self.extra)

    def shift(self, strength, g, j):
        row = HALO * g + j + self.fact_row
        return strength * self.heat[row : row + 1, :]


def rows_from(ref, row):
    return lambda g: ref.at[pl.ds(HALO * g + row, HALO)]


def fetch_all(plan, where):
    seen = set()
    for tasks in plan:
        for _, g in tasks:
            if g not in seen:
                seen.add(g)
                where(g).fetch(g)


def advance(plan, where, shift, strength, vectors, direction, residual, total):
    scalars = chebyshev_scalars()
    for tasks in plan:
        k = tasks[0][0]
        keep, gain = scalars[k - 1]
        products = []
        for _, g in tasks:
            where(g).wait(g)
            products += [where(g).product(vectors[k - 1], g, j) for j in range(HALO)]
        for n, (_, g) in enumerate(tasks):
            for j in range(HALO):
                product, state = products[n * HALO + j], HALO * g + j + shift
                diag = where(g).diagonal(product, g, j)
                v = direction[state]
                mv = diag * v - product[:COMPS, :] + where(g).shift(strength, g, j) * rotated(v)
                r = residual[state] - mv
                new = keep * v + gain * r / diag
                total[state] = total[state] + new
                if k < STEPS:
                    residual[state] = r
                    direction[state] = new
                    vectors[k][HALO + state] = with_ones(new)


def split(refs, rows):
    vectors, fields = refs
    places = rows + 2 * HALO + 1
    return (
        [vectors.at[pl.ds(k * places, places)] for k in range(STEPS)],
        *[fields.at[pl.ds(n * rows, rows)] for n in range(3)],
    )


def state_shape(rows):
    return [
        ((STEPS * (rows + 2 * HALO + 1), 2 * COMPS, TILE), BF16),
        ((3 * rows, COMPS, TILE), F32),
    ]


def clear(fields, vectors, blank_place, blank_places):
    zero = jnp.zeros((COMPS, TILE), F32)

    def body(i, carry):
        fields[i] = zero
        return carry

    lax.fori_loop(0, fields.shape[0], body, 0)
    for k, vector in enumerate(vectors):
        vector[blank_place] = jnp.zeros((2 * COMPS, TILE), BF16)
        for place in blank_places(k):
            vector[place] = with_ones(zero)


FAST = 6


def first_kernel(plan, table, group, own, near, far, opposite, diag, film, heat, fast_hbm, tiles_hbm,
                 surface, vectors, fields, fast_buffer, slow_buffer, sems):
    vector, direction, residual, total = split((vectors, fields), HEAD_ROWS)
    groups = range(HEAD // HALO)
    fast = Rows(groups[:FAST], 0, True, rows_from(fast_hbm, 0), fast_buffer, sems, table, film, heat, 0, 0)
    slow = Rows(groups[FAST:], FAST, False, rows_from(tiles_hbm, 0), slow_buffer, sems, table, film, heat, 0, 0)

    def where(g):
        return fast if g < FAST else slow

    fetch_all(plan, where)

    def blank_places(k):
        above = HALO + LEND + SURF_TILES + HALO * k
        below = HALO + LEND - HALO * (k + 2)
        places = [0] + [above + j for j in range(2 * HALO)]
        return places + [below + j for j in range(2 * HALO) if 0 <= below + j < HALO + LEND]

    clear(fields, vector, HEAD_BLANK, blank_places)
    for shift, part in enumerate((own, near, far, opposite)):
        g = lax.rem(group[0] + 4 - shift, 4)
        surface[:, pl.ds(pl.multiple_of(g * SUB, SUB), SUB)] = part[...]
        for j in range(HALO):
            value = part[:, j * TILE : (j + 1) * TILE]
            i = g * HALO + j
            new = value / (CENTRE * diag[i])
            residual[LEND + i] = value
            direction[LEND + i] = new
            total[LEND + i] = new
            vector[0][HALO + LEND + i] = with_ones(new)
    advance(plan, where, LEND, strengths(group[0]), vector, direction, residual, total)


def second_kernel(plan, table, lent_table, place, group, film, heat, facts, vectors_in, fields_in, fast_hbm,
                  *rest):
    lent_hbm, rest = rest[: len(PIECES)], rest[len(PIECES) :]
    head, edge, vectors, fields, fast_buffer, lent_buffer, sems = rest
    vector, direction, residual, total = split((vectors, fields), HEAD_ROWS)
    first = (place[0] == 0).astype(F32)
    lent_groups = range(-LEND // HALO, 0)

    def lent_rows(g):
        row = HALO * g + LEND
        for piece, count in zip(lent_hbm, PIECES):
            if row < count:
                return piece.at[pl.ds(row, HALO)]
            row -= count

    lent = Rows(lent_groups, FAST, False, lent_rows, lent_buffer, sems, lent_table,
                facts.at[pl.ds(SLOTS, LEND)], facts.at[pl.ds(SLOTS + LEND, LEND)], LEND,
                table.shape[1], first)
    fast = Rows(range(FAST), 0, True, rows_from(fast_hbm, 0), fast_buffer, sems, table, film, heat, 0, 0)

    def where(g):
        return lent if g < 0 else fast

    fetch_all(plan, where)
    vectors[...] = vectors_in[...]
    fields[...] = fields_in[...]
    advance(plan, where, LEND, strengths(group[0]), vector, direction, residual, total)
    for k in range(0, STEPS, 2):
        for j in range(HALO):
            i = HALO + LEND + j
            a = vector[k][i].astype(F32)[:COMPS]
            b = vector[k + 1][i].astype(F32)[:COMPS] if k + 1 < STEPS else a
            edge[k // 2, j] = jnp.concatenate([a, b], axis=0).astype(BF16)
    for j in range(HEAD):
        head[:, j * TILE : (j + 1) * TILE] = total[LEND + j]


def tail_kernel(plan, table, group, edge, film, heat, head, tiles_hbm, out, vectors, fields, buffer, sems):
    vector, direction, residual, total = split((vectors, fields), TAIL)
    row_tiles = out.shape[1] // TILE
    first = row_tiles - TAIL
    rows = Rows(range(-TAIL // HALO, 0), 0, False, rows_from(tiles_hbm, row_tiles), buffer, sems, table, film, heat,
                row_tiles, row_tiles)

    def where(g):
        return rows

    fetch_all(plan, where)

    def blank_places(k):
        below = HALO + TAIL - HALO * (k + 2)
        return [below + j for j in range(2 * HALO)]

    clear(fields, vector, TAIL_BLANK, blank_places)
    for k in range(STEPS):
        for j in range(HALO):
            pair = edge[k // 2, j].astype(F32)
            half = pair[(k % 2) * COMPS : (k % 2 + 1) * COMPS, :]
            vector[k][HALO + TAIL + j] = with_ones(half)
    out[:, : HEAD * TILE] = head[...]
    out[:, HEAD * TILE : first * TILE] = jnp.zeros((COMPS, (first - HEAD) * TILE), F32)
    advance(plan, where, TAIL, strengths(group[0]), vector, direction, residual, total)
    for j in range(TAIL):
        out[:, (first + j) * TILE : (first + j + 1) * TILE] = total[j]


def vmem():
    return pl.BlockSpec(memory_space=pltpu.VMEM)


def smem():
    return pl.BlockSpec(memory_space=pltpu.SMEM)


def hbm():
    return pl.BlockSpec(memory_space=pltpu.HBM)


def in_hbm(*arrays):
    return [pltpu.with_memory_space_constraint(a, pltpu.HBM) for a in arrays]


def work(gigaflops):
    return pl.CostEstimate(flops=gigaflops * 10**9, bytes_accessed=0, transcendentals=0)


def kernel_params(mib):
    return pltpu.CompilerParams(vmem_limit_bytes=mib << 20)


def local(
    boundary_power_density,
    face_scales,
    face_node,
    send_counts,
    tile_values,
    tile_mask,
    tile_columns,
    film_sink,
    capacity,
):
    parts = lax.axis_size("space")
    groups = lax.axis_size("freq")
    place = lax.axis_index("space")
    group = lax.axis_index("freq").astype(jnp.int32).reshape(1)
    nodes_here = film_sink.shape[0]
    row_tiles = nodes_here // TILE
    up = [(i, i + 1) for i in range(parts - 1)]
    down = [(i + 1, i) for i in range(parts - 1)]
    first_plan, second_plan = head_plan()
    assert groups == 4

    tile_values = pltpu.with_memory_space_constraint(tile_values, pltpu.HBM)
    film = film_sink.reshape(row_tiles, TILE)
    heat = capacity.reshape(row_tiles, TILE)
    columns, mask = tile_columns.T, tile_mask.T

    def array(shape, dtype=F32):
        return jax.ShapeDtypeStruct(shape, dtype)

    packed, head_table, tail_table, facts = pl.pallas_call(
        pack_kernel,
        out_shape=(
            array((parts, PACK, TILE), BF16),
            array((SLOTS, row_tiles), jnp.int32),
            array((SLOTS, row_tiles), jnp.int32),
            array((SLOTS + 2 * LEND, TILE)),
        ),
        in_specs=[smem()] + [vmem()] * 7,
        out_specs=(vmem(),) * 4,
        compiler_params=kernel_params(8),
        name="pack",
    )(
        send_counts,
        *in_hbm(
            boundary_power_density,
            face_scales.reshape(parts, TILE),
            face_node.reshape(parts, TILE),
            columns,
            mask,
            film,
            heat,
        ),
    )
    got = lax.all_to_all(packed, "space", 0, 0)

    facts = lax.ppermute(facts, "space", up)
    lent = pl.pallas_call(
        lend_kernel,
        out_shape=[array((count, SLOTS, TILE, TILE), BF16) for count in PIECES],
        in_specs=[hbm()],
        out_specs=[vmem()] * len(PIECES),
        scratch_shapes=[pltpu.SemaphoreType.DMA((len(PIECES),))],
        compiler_params=kernel_params(8),
        cost_estimate=pl.CostEstimate(flops=0, bytes_accessed=6 << 20, transcendentals=0),
        name="lend",
    )(tile_values)
    lent = [lax.ppermute(piece, "space", up) for piece in lent]
    lent_table = facts[:SLOTS].astype(jnp.int32)

    depth = 4
    fast_tiles, diag = pl.pallas_call(
        prep_kernel,
        out_shape=(
            pltpu.HBM((FAST * HALO, SLOTS, TILE, TILE), BF16),
            array((SURF_TILES, COMPS, TILE)),
        ),
        in_specs=[smem(), vmem(), hbm()],
        out_specs=(hbm(), vmem()),
        scratch_shapes=[
            pltpu.VMEM((depth, HALO, SLOTS, TILE, TILE), BF16),
            pltpu.VMEM((FAST * HALO, SLOTS, TILE, TILE), BF16),
            pltpu.SemaphoreType.DMA((depth,)),
            pltpu.SemaphoreType.DMA((FAST,)),
        ],
        compiler_params=kernel_params(16),
        cost_estimate=pl.CostEstimate(flops=0, bytes_accessed=12 << 20, transcendentals=0),
        name="prep",
    )(mask, film, tile_values)

    (fast_tiles,) = in_hbm(fast_tiles)
    parts_of = pl.pallas_call(
        scatter_kernel,
        out_shape=(array((COMPS, SUB)),) * groups,
        in_specs=[smem(), vmem(), vmem()],
        out_specs=(vmem(),) * groups,
        scratch_shapes=[pltpu.VMEM((LEVELS, SUB), F32)] * 2,
        compiler_params=kernel_params(8),
        name="scatter",
    )(group, jnp.asarray(fourier_table()), got)
    mixed = [parts_of[0]] + [
        lax.ppermute(parts_of[s], "freq", [(i, (i + s) % groups) for i in range(groups)])
        for s in range(1, groups)
    ]

    held = state_shape(HEAD_ROWS)
    groups_here = HEAD // HALO

    def tile_buffer(count):
        return pltpu.VMEM((count * HALO, SLOTS, TILE, TILE), BF16)

    surface, *state = pl.pallas_call(
        lambda *refs: first_kernel(first_plan, *refs),
        out_shape=(array((COMPS, SURF_TILES * TILE)), *[array(*h) for h in held]),
        in_specs=[smem()] * 2 + [vmem()] * 7 + [hbm()] * 2,
        out_specs=(vmem(),) * 3,
        scratch_shapes=[
            tile_buffer(FAST),
            tile_buffer(groups_here - FAST),
            pltpu.SemaphoreType.DMA((groups_here,)),
        ],
        compiler_params=kernel_params(24),
        cost_estimate=work(200),
        name="first",
    )(head_table, group, *mixed, diag, film, heat, fast_tiles, tile_values)

    head, edge = pl.pallas_call(
        lambda *refs: second_kernel(second_plan, *refs),
        out_shape=(
            array((COMPS, HEAD * TILE)),
            array(((STEPS + 1) // 2, HALO, 2 * COMPS, TILE), BF16),
        ),
        in_specs=[smem()] * 4 + [vmem()] * 5 + [hbm()] * (1 + len(PIECES)),
        out_specs=(vmem(),) * 2,
        scratch_shapes=[
            *[pltpu.VMEM(*h) for h in held],
            tile_buffer(FAST),
            tile_buffer(LEND // HALO),
            pltpu.SemaphoreType.DMA((FAST + LEND // HALO,)),
        ],
        compiler_params=kernel_params(24),
        name="second",
    )(
        head_table,
        lent_table,
        place.astype(jnp.int32).reshape(1),
        group,
        film,
        heat,
        facts,
        *state,
        fast_tiles,
        *lent,
    )
    edge = lax.ppermute(edge, "space", down)

    temperature = pl.pallas_call(
        lambda *refs: tail_kernel(tail_plan(), *refs),
        out_shape=array((COMPS, nodes_here)),
        in_specs=[smem()] * 2 + [vmem()] * 4 + [hbm()],
        out_specs=vmem(),
        scratch_shapes=[
            *[pltpu.VMEM(*h) for h in state_shape(TAIL)],
            tile_buffer(TAIL // HALO),
            pltpu.SemaphoreType.DMA((TAIL // HALO,)),
        ],
        compiler_params=kernel_params(24),
        name="tail",
    )(tail_table, group, edge, film, heat, head, tile_values)
    return surface, temperature


def solution(mesh):
    placed = (
        P(None, ("freq", "space")),
        P(("freq", "space")),
        P(("freq", "space")),
        P(("freq", "space")),
        P("space", None, None, None),
        P("space", None),
        P("space", None),
        P("space"),
        P("space"),
    )
    return jax.shard_map(
        local,
        mesh=mesh,
        in_specs=placed,
        out_specs=(P("freq", "space"), P("freq", "space")),
        check_vma=False,
    )
```

time: 401 us -> 84.4 us (0.21)
  matrix products: 124 us -> 0 us
  waiting for transfers between devices: 96.9 us -> 14.3 us
  other arithmetic: 56.6 us -> 0.01 us
  local copies, waits for them, and re-layouts: 55.1 us -> 0.67 us
  Pallas kernels: 0 us -> 46.4 us
  starting transfers between devices: 39.6 us -> 21.6 us
  between operations: 14.7 us -> 0.97 us
  blocking collectives: 12.4 us -> 0 us
    dot_general x9 -> x0, matrix products: 124 us -> none  [the longest x7 109 us: couple(): jnp.einsum('crtj,rtij->cri', picked, tiles, preferred_element_type=jnp.fl...]
    reduce_scatter x1 -> x0, waiting for transfers between devices: 75.9 us -> none  [local(): lax.psum_scatter(dense_sums, 'space', scatter_dimension=1, tiled=True)]
    pallas_call x0 -> x7, Pallas kernels: none -> 46.4 us  [the longest x1 11.5 us: local(): pl.pallas_call(lambda *refs: first_kernel(first_plan, *refs), out_shape=(...]
    gather x9 -> x0, local copies, waits for them, and re-layouts: 44.2 us -> none  [the longest x7 40.3 us: couple(): picked = blocks[:, columns] * mask_bf[None, :, :, None]]
    scatter-add x1 -> x0, other arithmetic: 26.1 us -> none  [local(): dense_sums = jnp.zeros((thermal_states, spatial_extent * BOUNDARY_PER_CPU...]
    ppermute x14 -> x6, starting transfers between devices: 39.6 us -> 14.1 us  [the longest x3 5.06 us: local(): lax.ppermute(parts_of[s], 'freq', [(i, (i + s) % groups) for i in range(g...]
    convert_element_type x3 -> x1, other arithmetic: 16.5 us -> 0.01 us  [local(): lent_table = facts[:SLOTS].astype(jnp.int32)]
    all_gather x1 -> x0, blocking collectives: 12.4 us -> none  [local(): gathered = lax.all_gather(level_sums, 'freq', axis=1, tiled=True)]
  transfers between devices with their start and end apart: 15 -> 7, of which waited for: 8 -> 4; matrix products, arithmetic and copies ran while one was open for 7% -> 0% of each run, Pallas kernels for 0% -> 28%
where the time goes in v2:
time: 84.4 us; the launch traced here: 83.9 us
  Pallas kernels  46.4 us (55%)
  starting transfers between devices  21.6 us (26%)
  waiting for transfers between devices  14.3 us (17%)
  between operations  0.97 us (1%)
    pallas_call x1, Pallas kernels, local(): pl.pallas_call(lambda *refs: first_kernel(first_plan, *refs), out_shape=(...  11.5 us
    pallas_call x1, Pallas kernels, local(): pl.pallas_call(lambda *refs: tail_kernel(tail_plan(), *refs), out_shape=a...  11.2 us
    pallas_call x1, Pallas kernels, local(): pl.pallas_call(lambda *refs: second_kernel(second_plan, *refs), out_shape...  9.79 us
    ppermute x1, waiting for transfers between devices, local(): lent = [lax.ppermute(piece, 'space', up) for piece in lent]  7.54 us
    all_to_all x1, starting transfers between devices, local(): got = lax.all_to_all(packed, 'space', 0, 0)  7.44 us
    pallas_call x1, Pallas kernels, local(): pl.pallas_call(prep_kernel, out_shape=(pltpu.HBM((FAST * HALO, SLOTS, TIL...  6.45 us
    ppermute x3, starting transfers between devices, local(): lax.ppermute(parts_of[s], 'freq', [(i, (i + s) % groups) for i in range(g...  5.06 us
    ppermute x1, waiting for transfers between devices, local(): edge = lax.ppermute(edge, 'space', down)  4.89 us
  transfers between devices with their start and end apart: 7, of which 4 were waited for; matrix products, arithmetic and copies ran while one was open for 0% of the time, Pallas kernels for 28%

profile of v2, /device:TPU:97, one launch (start us, length us, event | category | flops | bytes accessed | tf_op | source)
XLA Modules:
  0.0 83.9 jit_solution(3301174032432531129)
XLA Ops:
  0.6 0.0 copy-start.4
  0.6 0.6 copy-done.4
  1.3 1.9 %pack.1 = (bf16[32,48,128]{2,1,0:T(8,128)(2,1)}, s32[8,128]{1,0:T(8,128)S(1)}, s32[8,128]{1,0:T(8,128)S(1)}, f32[32,128]{1,0:T(8,128)S(1)}) custom-call(s32[32]{0:T(128)S(1)} %copy-done.4, bf16[32,4096]{1,0:T(8,128)(2,1)} %power.1, bf16[32,128]{1,0:T(8,128)(2,1)} %bitcast.20, s32[32,128]{1,0:T(8,128)} %bitcast.19, s32[8,128]{1,0:T(8,128)} %bitcast.21, ...), custom_call_target="tpu_custom_call" | custom-call | tf_op jit(solution)/shard_map/pack/pallas_call | solution.py:498
  3.1 7.4 %all-to-all-start = ((bf16[32,48,128]{2,1,0:T(8,128)(2,1)}), bf16[32,48,128]{2,1,0:T(8,128)(2,1)S(1)}, u32[]{:S(2)}, u32[]{:S(2)}) async-start(bf16[32,48,128]{2,1,0:T(8,128)(2,1)} %get-tuple-element.18), calls=%async_computation | async-start | bytes 786432 | tf_op jit(solution)/shard_map/all_to_all | solution.py:522
  10.6 0.0 copy-start
  10.6 0.0 copy-start.3
  10.6 3.5 %collective-permute-start.3 = (f32[32,128]{1,0:T(8,128)S(1)}, f32[32,128]{1,0:T(8,128)S(1)}, u32[]{:S(2)}, u32[]{:S(2)}) collective-permute-start(f32[32,128]{1,0:T(8,128)S(1)} %get-tuple-element.27), channel_id=1, source_target_pairs={{0,1},{1,2},{2,3},{3,4},{4,5},{5,6},{6,7},{7,8},{8,9},{9,10},{10,1... | collective-permute-start | bytes 49160 | tf_op jit(solution)/shard_map/ppermute | solution.py:524
  14.1 3.6 %lend.1 = bf16[12,8,128,128]{3,2,1,0:T(8,128)(2,1)} custom-call(bf16[128,8,128,128]{3,2,1,0:T(8,128)(2,1)} %refs_6_.1), custom_call_target="tpu_custom_call" | custom-call | bytes 6291456 | tf_op jit(solution)/shard_map/lend/pallas_call | solution.py:525
  17.7 2.1 %collective-permute-start.4 = (bf16[12,8,128,128]{3,2,1,0:T(8,128)(2,1)}, bf16[12,8,128,128]{3,2,1,0:T(8,128)(2,1)}, u32[]{:S(2)}, u32[]{:S(2)}) collective-permute-start(bf16[12,8,128,128]{3,2,1,0:T(8,128)(2,1)} %lend.1), channel_id=1, source_target_pairs={{0,1},{1,2},{2,3},{3,4},{4,5},{5,6},{6,7},{7,8},{8,9},{9,10},{10,1... | collective-permute-start | bytes 9437192 | tf_op jit(solution)/shard_map/ppermute | solution.py:535
  19.8 0.0 copy-done
  19.8 0.0 copy-done.3
  19.8 0.0 copy-start.2
  19.8 0.0 copy-start.1
  19.8 6.5 %prep.1 = (bf16[24,8,128,128]{3,2,1,0:T(8,128)(2,1)}, f32[16,8,128]{2,1,0:T(8,128)S(1)}) custom-call(s32[8,128]{1,0:T(8,128)S(1)} %bitcast.18, f32[128,128]{1,0:T(8,128)S(1)} %bitcast.9, bf16[128,8,128,128]{3,2,1,0:T(8,128)(2,1)} %refs_6_.1), custom_call_target="tpu_custom_call" | custom-call | bytes 12582912 | tf_op jit(solution)/shard_map/prep/pallas_call | solution.py:539
  26.3 0.0 all-to-all-done.got
  26.3 0.0 copy-done.2
  26.3 1.9 %scatter.1 = (f32[8,512]{1,0:T(8,128)S(1)}, f32[8,512]{1,0:T(8,128)S(1)}, f32[8,512]{1,0:T(8,128)S(1)}, f32[8,512]{1,0:T(8,128)S(1)}) custom-call(s32[1]{0:T(128)} %bitcast.6.group.refs_1_.refs_3_, f32[32,32]{1,0:T(8,128)S(1)} %copy-done.2, bf16[32,48,128]{2,1,0:T(8,128)(2,1)S(1)} %all-to-all-done.got), custom_call_target="tpu_custom_call" | custom-call | tf_op jit(solution)/shard_map/scatter/pallas_call | solution.py:559
  28.3 1.4 %collective-permute-start = (f32[8,512]{1,0:T(8,128)S(1)}, f32[8,512]{1,0:T(8,128)S(1)}, u32[]{:S(2)}, u32[]{:S(2)}) collective-permute-start(f32[8,512]{1,0:T(8,128)S(1)} %get-tuple-element.20), channel_id=1, source_target_pairs={{0,32},{32,64},{64,96},{96,0},{1,33},{33,65},{65,97},{97,1},{2,34}... | collective-permute-start | bytes 49160 | tf_op jit(solution)/shard_map/ppermute | solution.py:569
  29.6 2.6 %collective-permute-start.1 = (f32[8,512]{1,0:T(8,128)S(1)}, f32[8,512]{1,0:T(8,128)S(1)}, u32[]{:S(2)}, u32[]{:S(2)}) collective-permute-start(f32[8,512]{1,0:T(8,128)S(1)} %get-tuple-element.21), channel_id=1, source_target_pairs={{0,64},{32,96},{64,0},{96,32},{1,65},{33,97},{65,1},{97,33},{2,66}... | collective-permute-start | bytes 49160 | tf_op jit(solution)/shard_map/ppermute | solution.py:569
  32.2 1.1 %collective-permute-start.2 = (f32[8,512]{1,0:T(8,128)S(1)}, f32[8,512]{1,0:T(8,128)S(1)}, u32[]{:S(2)}, u32[]{:S(2)}) collective-permute-start(f32[8,512]{1,0:T(8,128)S(1)} %get-tuple-element.22), channel_id=1, source_target_pairs={{0,96},{32,0},{64,32},{96,64},{1,97},{33,1},{65,33},{97,65},{2,98}... | collective-permute-start | bytes 49160 | tf_op jit(solution)/shard_map/ppermute | solution.py:569
  33.3 0.0 collective-permute-done.3.refs_6_
  33.3 0.0 collective-permute-done.refs_3_
  33.3 0.4 collective-permute-done.1.refs_4_
  33.7 1.5 %collective-permute-done.2.refs_5_ = f32[8,512]{1,0:T(8,128)S(1)} collective-permute-done((f32[8,512]{1,0:T(8,128)S(1)}, f32[8,512]{1,0:T(8,128)S(1)}, u32[]{:S(2)}, u32[]{:S(2)}) %collective-permute-start.2) | collective-permute-done | bytes 16416 | tf_op jit(solution)/shard_map/ppermute | solution.py:569
  35.2 0.0 copy-done.1
  35.2 11.5 %first.1 = (f32[8,2048]{1,0:T(8,128)}, bf16[455,16,128]{2,1,0:T(8,128)(2,1)S(1)}, f32[168,8,128]{2,1,0:T(8,128)S(1)}) custom-call(s32[8,128]{1,0:T(8,128)S(1)} %get-tuple-element.17.refs_0_, s32[1]{0:T(128)} %bitcast.6.group.refs_1_.refs_3_, f32[8,512]{1,0:T(8,128)S(1)} %get-tuple-element.19.refs_2_, f32[8,512]{1,0:T(8,128)S(1)} %collective-permute-done.refs_3_, ...), custom_call_target="tpu_custom_call" | custom-call | flops 199999995904 | tf_op jit(solution)/shard_map/first/pallas_call | solution.py:579
  46.7 7.5 %collective-permute-done.4.refs_10_ = bf16[12,8,128,128]{3,2,1,0:T(8,128)(2,1)} collective-permute-done((bf16[12,8,128,128]{3,2,1,0:T(8,128)(2,1)}, bf16[12,8,128,128]{3,2,1,0:T(8,128)(2,1)}, u32[]{:S(2)}, u32[]{:S(2)}) %collective-permute-start.4) | collective-permute-done | bytes 3145760 | tf_op jit(solution)/shard_map/ppermute | solution.py:535
  54.3 9.8 %second.1 = (f32[8,5632]{1,0:T(8,128)S(1)}, bf16[4,4,16,128]{3,2,1,0:T(8,128)(2,1)S(1)}) custom-call(s32[8,128]{1,0:T(8,128)S(1)} %get-tuple-element.17.refs_0_, s32[8,128]{1,0:T(8,128)S(1)} %slice_convert_fusion.refs_1_, s32[1]{0:T(128)} %bitcast.7.refs_2_, s32[1]{0:T(128)} %bitcast.6.group.refs_1_.refs_3_, f32[128,128]{1,0:T(8,128)S(1)} %bitcast.11, ...), custom_call_target="tpu_custom_call" | custom-call | tf_op jit(solution)/shard_map/second/pallas_call | solution.py:594
  64.1 3.5 %collective-permute-start.5 = (bf16[4,4,16,128]{3,2,1,0:T(8,128)(2,1)S(1)}, bf16[4,4,16,128]{3,2,1,0:T(8,128)(2,1)S(1)}, u32[]{:S(2)}, u32[]{:S(2)}) collective-permute-start(bf16[4,4,16,128]{3,2,1,0:T(8,128)(2,1)S(1)} %get-tuple-element.30), channel_id=1, source_target_pairs={{1,0},{2,1},{3,2},{4,3},{5,4},{6,5},{7,6},{8,7},{9,8},{10,9},{11,1... | collective-permute-start | bytes 196616 | tf_op jit(solution)/shard_map/ppermute | solution.py:622
  67.6 4.9 %collective-permute-done.5.refs_2_ = bf16[4,4,16,128]{3,2,1,0:T(8,128)(2,1)S(1)} collective-permute-done((bf16[4,4,16,128]{3,2,1,0:T(8,128)(2,1)S(1)}, bf16[4,4,16,128]{3,2,1,0:T(8,128)(2,1)S(1)}, u32[]{:S(2)}, u32[]{:S(2)}) %collective-permute-start.5) | collective-permute-done | bytes 65568 | tf_op jit(solution)/shard_map/ppermute | solution.py:622
  72.5 11.2 %tail.1 = f32[8,16384]{1,0:T(8,128)} custom-call(s32[8,128]{1,0:T(8,128)S(1)} %get-tuple-element.26.refs_0_, s32[1]{0:T(128)} %bitcast.6.group.refs_1_.refs_3_, bf16[4,4,16,128]{3,2,1,0:T(8,128)(2,1)S(1)} %collective-permute-done.5.refs_2_, f32[128,128]{1,0:T(8,128)S(1)} %bitcast.12, f32[128,128]{1,0:T(8,128)S(1)} %bitcast.16, ...), custom_call_target="tpu_custom_call" | custom-call | tf_op jit(solution)/shard_map/tail/pallas_call | solution.py:624
  (1 shorter events, 0.0 us)
Async XLA Ops:
  0.6 0.7 copy-start.4
  3.1 23.1 %all-to-all-start = ((bf16[32,48,128]{2,1,0:T(8,128)(2,1)}), bf16[32,48,128]{2,1,0:T(8,128)(2,1)S(1)}, u32[]{:S(2)}, u32[]{:S(2)}) async-start(bf16[32,48,128]{2,1,0:T(8,128)(2,1)} %get-tuple-element.18), calls=%async_computation | async-start | bytes 786432 | tf_op jit(solution)/shard_map/all_to_all | solution.py:522
  10.6 9.2 %copy-start = (f32[16384]{0:T(1024)S(1)}, f32[16384]{0:T(1024)}, u32[]{:S(2)}) copy-start(f32[16384]{0:T(1024)} %param.17) | copy-start | bytes 196612
  10.6 9.2 %copy-start.3 = (s32[128,8]{0,1:T(8,128)S(1)}, s32[128,8]{0,1:T(8,128)}, u32[]{:S(2)}) copy-start(s32[128,8]{0,1:T(8,128)} %param.15) | copy-start | bytes 12292
  10.6 22.7 %collective-permute-start.3 = (f32[32,128]{1,0:T(8,128)S(1)}, f32[32,128]{1,0:T(8,128)S(1)}, u32[]{:S(2)}, u32[]{:S(2)}) collective-permute-start(f32[32,128]{1,0:T(8,128)S(1)} %get-tuple-element.27), channel_id=1, source_target_pairs={{0,1},{1,2},{2,3},{3,4},{4,5},{5,6},{6,7},{7,8},{8,9},{9,10},{10,1... | collective-permute-start | bytes 49160 | tf_op jit(solution)/shard_map/ppermute | solution.py:524
  17.7 36.6 %collective-permute-start.4 = (bf16[12,8,128,128]{3,2,1,0:T(8,128)(2,1)}, bf16[12,8,128,128]{3,2,1,0:T(8,128)(2,1)}, u32[]{:S(2)}, u32[]{:S(2)}) collective-permute-start(bf16[12,8,128,128]{3,2,1,0:T(8,128)(2,1)} %lend.1), channel_id=1, source_target_pairs={{0,1},{1,2},{2,3},{3,4},{4,5},{5,6},{6,7},{7,8},{8,9},{9,10},{10,1... | collective-permute-start | bytes 9437192 | tf_op jit(solution)/shard_map/ppermute | solution.py:535
  19.8 6.5 %copy-start.2 = (f32[32,32]{1,0:T(8,128)S(1)}, f32[32,32]{1,0:T(8,128)}, u32[]{:S(2)}) copy-start(f32[32,32]{1,0:T(8,128)} %constant.11.clone.table) | copy-start | bytes 12292
  19.8 15.4 %copy-start.1 = (f32[16384]{0:T(1024)S(1)}, f32[16384]{0:T(1024)}, u32[]{:S(2)}) copy-start(f32[16384]{0:T(1024)} %param.18) | copy-start | bytes 196612
  28.3 5.1 %collective-permute-start = (f32[8,512]{1,0:T(8,128)S(1)}, f32[8,512]{1,0:T(8,128)S(1)}, u32[]{:S(2)}, u32[]{:S(2)}) collective-permute-start(f32[8,512]{1,0:T(8,128)S(1)} %get-tuple-element.20), channel_id=1, source_target_pairs={{0,32},{32,64},{64,96},{96,0},{1,33},{33,65},{65,97},{97,1},{2,34}... | collective-permute-start | bytes 49160 | tf_op jit(solution)/shard_map/ppermute | solution.py:569
  29.6 4.1 %collective-permute-start.1 = (f32[8,512]{1,0:T(8,128)S(1)}, f32[8,512]{1,0:T(8,128)S(1)}, u32[]{:S(2)}, u32[]{:S(2)}) collective-permute-start(f32[8,512]{1,0:T(8,128)S(1)} %get-tuple-element.21), channel_id=1, source_target_pairs={{0,64},{32,96},{64,0},{96,32},{1,65},{33,97},{65,1},{97,33},{2,66}... | collective-permute-start | bytes 49160 | tf_op jit(solution)/shard_map/ppermute | solution.py:569
  32.2 3.0 %collective-permute-start.2 = (f32[8,512]{1,0:T(8,128)S(1)}, f32[8,512]{1,0:T(8,128)S(1)}, u32[]{:S(2)}, u32[]{:S(2)}) collective-permute-start(f32[8,512]{1,0:T(8,128)S(1)} %get-tuple-element.22), channel_id=1, source_target_pairs={{0,96},{32,0},{64,32},{96,64},{1,97},{33,1},{65,33},{97,65},{2,98}... | collective-permute-start | bytes 49160 | tf_op jit(solution)/shard_map/ppermute | solution.py:569
  64.1 8.4 %collective-permute-start.5 = (bf16[4,4,16,128]{3,2,1,0:T(8,128)(2,1)S(1)}, bf16[4,4,16,128]{3,2,1,0:T(8,128)(2,1)S(1)}, u32[]{:S(2)}, u32[]{:S(2)}) collective-permute-start(bf16[4,4,16,128]{3,2,1,0:T(8,128)(2,1)S(1)} %get-tuple-element.30), channel_id=1, source_target_pairs={{1,0},{2,1},{3,2},{4,3},{5,4},{6,5},{7,6},{8,7},{9,8},{10,9},{11,1... | collective-permute-start | bytes 196616 | tf_op jit(solution)/shard_map/ppermute | solution.py:622

commit v3 on v2

--- a/solution.py
+++ b/solution.py
@@ -25,7 +25,7 @@
 HEAD = SURF_TILES + HALO * STEPS
 TAIL = HALO * STEPS
 LEND = 12
-PIECES = (12,)
+AHEAD = 4
 PACK = 48
 
 HEAD_ROWS = LEND + HEAD
@@ -95,9 +95,24 @@
     return [[(k, g) for g in range(-k, 0)] for k in range(1, STEPS + 1)]
 
 
-def pack_kernel(counts, power, scales, nodes, columns, mask, film, heat, out, head_table, tail_table, facts):
+def copy_rows(tiles_hbm, first, out, sems):
+    copies = []
+    for n in range(out.shape[0]):
+        copies.append(pltpu.make_async_copy(tiles_hbm.at[first + n], out.at[n], sems.at[n]))
+        copies[-1].start()
+    return copies
+
+
+def lend_kernel(tiles_hbm, near, sems):
+    for copy in copy_rows(tiles_hbm, tiles_hbm.shape[0] - LEND + AHEAD, near, sems):
+        copy.wait()
+
+
+def pack_kernel(counts, power, scales, nodes, mask, columns, film, heat, tiles_hbm, out, head_table, tail_table,
+                facts, far, sems):
+    row_tiles = film.shape[0]
     targets = out.shape[0]
-    row_tiles = film.shape[0]
+    copies = copy_rows(tiles_hbm, row_tiles - LEND, far, sems)
     row = lax.broadcasted_iota(jnp.int32, (16, TILE), 0)
     lane = lax.broadcasted_iota(jnp.int32, (16, TILE), 1)
     for d in range(targets):
@@ -116,6 +131,8 @@
     facts[:SLOTS, :] = lent_table.astype(F32)
     facts[SLOTS : SLOTS + LEND, :] = film[row_tiles - LEND :, :]
     facts[SLOTS + LEND :, :] = heat[row_tiles - LEND :, :]
+    for copy in copies:
+        copy.wait()
 
 
 def scatter_kernel(group, table, got, *rest):
@@ -155,71 +172,6 @@
     return jnp.concatenate([v, jnp.ones((COMPS, TILE), F32)], axis=0).astype(BF16)
 
 
-def lend_kernel(tiles_hbm, *rest):
-    pieces, sems = rest[:-1], rest[-1]
-    first = tiles_hbm.shape[0] - sum(piece.shape[0] for piece in pieces)
-    copies = []
-    for n, piece in enumerate(pieces):
-        rows = pl.ds(first, piece.shape[0])
-        copies.append(pltpu.make_async_copy(tiles_hbm.at[rows], piece, sems.at[n]))
-        copies[-1].start()
-        first += piece.shape[0]
-    for copy in copies:
-        copy.wait()
-
-
-def transpose_tiles(first, tiles_hbm, out_hbm, buffer, tiles, sems, out_sem):
-    depth = buffer.shape[0]
-    chunks = tiles.shape[0] // HALO
-
-    def copy(q, slot):
-        return pltpu.make_async_copy(
-            tiles_hbm.at[pl.ds(first + q * HALO, HALO)], buffer.at[slot], sems.at[slot]
-        )
-
-    def back(q):
-        rows = pl.ds(q * HALO, HALO)
-        return pltpu.make_async_copy(tiles.at[rows], out_hbm.at[rows], out_sem.at[q])
-
-    for q in range(depth):
-        copy(q, q).start()
-
-    def chunk(q, carry):
-        slot = lax.rem(q, depth)
-        copy(q, slot).wait()
-        for j in range(HALO):
-            for t in range(SLOTS):
-                tiles[q * HALO + j, t] = buffer[slot, j, t].T
-        back(q).start()
-
-        @pl.when(q + depth < chunks)
-        def _():
-            copy(q + depth, slot).start()
-
-        return carry
-
-    lax.fori_loop(0, chunks, chunk, 0)
-    return [back(q) for q in range(chunks)]
-
-
-def prep_kernel(mask, film, tiles_hbm, out_hbm, diag, buffer, tiles, sems, out_sem):
-    copies = transpose_tiles(0, tiles_hbm, out_hbm, buffer, tiles, sems, out_sem)
-
-    def sums(i, carry):
-        rowsum = jnp.zeros((COMPS, TILE), F32)
-        for t in range(SLOTS):
-            tile = tiles[i, t].astype(F32).reshape(TILE // COMPS, COMPS, TILE)
-            rowsum += jnp.sum(tile, axis=0) * mask[t, i].astype(F32)
-        diag[i] = jnp.broadcast_to(
-            jnp.sum(rowsum, axis=0, keepdims=True) + film[pl.ds(i, 1), :], (COMPS, TILE)
-        )
-        return carry
-
-    lax.fori_loop(0, SURF_TILES, sums, 0)
-    for copy in copies:
-        copy.wait()
-
-
 def rotated(v):
     even = lax.broadcasted_iota(jnp.int32, v.shape, 0) % 2 == 0
     return jnp.where(even, -pltpu.roll(v, COMPS - 1, 0), pltpu.roll(v, 1, 0))
@@ -231,36 +183,45 @@
 
 
 class Rows:
-    def __init__(self, groups, first, transposed, source, buffer, sems, table, film, heat, fact_row, table_row,
-                 extra=0.0):
-        self.transposed, self.table, self.film, self.heat = transposed, table, film, heat
-        self.first, self.fact_row, self.table_row, self.extra = first, fact_row, table_row, extra
-        self.buffer, self.slot, self.copies = buffer, {}, {}
-        for n, g in enumerate(groups):
-            rows = pl.ds(n * HALO, HALO)
-            self.slot[g] = n * HALO
-            self.copies[g] = pltpu.make_async_copy(source(g), buffer.at[rows], sems.at[first + n])
+    def __init__(self, groups, table, film, heat, fact_row, table_row, extra=0.0, source=None, buffer=None,
+                 sems=None, turned=None, turned_groups=(), ready=()):
+        self.table, self.film, self.heat = table, film, heat
+        self.fact_row, self.table_row, self.extra = fact_row, table_row, extra
+        self.buffer, self.turned, self.ready = buffer, turned, set(ready)
+        self.turned_slot = {g: n * HALO for n, g in enumerate(turned_groups)}
+        self.slot, self.copies = {}, {}
+        if source is not None:
+            for n, g in enumerate(groups):
+                self.slot[g] = n * HALO
+                self.copies[g] = pltpu.make_async_copy(
+                    source(g), buffer.at[pl.ds(n * HALO, HALO)], sems.at[n]
+                )
 
     def fetch(self, g):
-        self.copies[g].start()
+        if g in self.copies:
+            self.copies[g].start()
 
     def wait(self, g):
         copy = self.copies.pop(g, None)
         if copy is not None:
             copy.wait()
 
+    def turn(self, g, j):
+        for t in range(SLOTS):
+            self.turned[self.turned_slot[g] + j, t] = self.buffer[self.slot[g] + j, t].T
+
     def product(self, vector, g, j):
-        i = self.slot[g] + j
         row = HALO * g + j + self.table_row
         left = jnp.concatenate([vector[self.table[t, row]] for t in range(SLOTS)], axis=1)
-        right = jnp.concatenate(
-            [self.buffer[i, t] for t in range(SLOTS)], axis=0 if self.transposed else 1
-        )
+        if g in self.ready:
+            i = self.turned_slot[g] + j
+            right = jnp.concatenate([self.turned[i, t] for t in range(SLOTS)], axis=0)
+        else:
+            i = self.slot[g] + j
+            right = jnp.concatenate([self.buffer[i, t] for t in range(SLOTS)], axis=1)
+        side = 0 if g in self.ready else 1
         return lax.dot_general(
-            left,
-            right,
-            (((1,), (0 if self.transposed else 1,)), ((), ())),
-            preferred_element_type=F32,
+            left, right, (((1,), (side,)), ((), ())), preferred_element_type=F32
         )
 
     def diagonal(self, product, g, j):
@@ -285,15 +246,28 @@
                 where(g).fetch(g)
 
 
-def advance(plan, where, shift, strength, vectors, direction, residual, total):
+def advance(plan, where, shift, strength, vectors, direction, residual, total, keep_turned=(), rate=2):
     scalars = chebyshev_scalars()
-    for tasks in plan:
+    for n_step, tasks in enumerate(plan):
         k = tasks[0][0]
         keep, gain = scalars[k - 1]
+        later = [g for step in plan[n_step + 1 :] for _, g in step] + list(keep_turned)
+        fetched = {g for step in plan[: n_step + 1] for _, g in step}
+        wanted = [
+            g for g in fetched if g in later and g in where(g).turned_slot and g not in where(g).ready
+        ]
+        wanted = sorted(wanted, key=lambda g: -later.count(g))[:rate]
+        turns = [(g, j) for g in wanted for j in range(HALO)]
         products = []
-        for _, g in tasks:
+        for n, (_, g) in enumerate(tasks):
             where(g).wait(g)
             products += [where(g).product(vectors[k - 1], g, j) for j in range(HALO)]
+            share = -(-len(turns) // len(tasks))
+            for h, j in [t for t in turns[n * share : (n + 1) * share]]:
+                where(h).wait(h)
+                where(h).turn(h, j)
+        for g in wanted:
+            where(g).ready.add(g)
         for n, (_, g) in enumerate(tasks):
             for j in range(HALO):
                 product, state = products[n * HALO + j], HALO * g + j + shift
@@ -307,6 +281,10 @@
                     residual[state] = r
                     direction[state] = new
                     vectors[k][HALO + state] = with_ones(new)
+    for g in keep_turned:
+        if g not in where(g).ready:
+            for j in range(HALO):
+                where(g).turn(g, j)
 
 
 def split(refs, rows):
@@ -340,17 +318,19 @@
 
 
 FAST = 6
-
-
-def first_kernel(plan, table, group, own, near, far, opposite, diag, film, heat, fast_hbm, tiles_hbm,
-                 surface, vectors, fields, fast_buffer, slow_buffer, sems):
+TURNED = 9
+
+
+def first_kernel(plan, table, group, own, near, far, opposite, film, heat, tiles_hbm, after, surface, vectors, fields,
+                 turned, buffer, sems):
+    del after
     vector, direction, residual, total = split((vectors, fields), HEAD_ROWS)
     groups = range(HEAD // HALO)
-    fast = Rows(groups[:FAST], 0, True, rows_from(fast_hbm, 0), fast_buffer, sems, table, film, heat, 0, 0)
-    slow = Rows(groups[FAST:], FAST, False, rows_from(tiles_hbm, 0), slow_buffer, sems, table, film, heat, 0, 0)
+    rows = Rows(groups, table, film, heat, 0, 0, source=rows_from(tiles_hbm, 0), buffer=buffer, sems=sems,
+                turned=turned, turned_groups=groups[:TURNED])
 
     def where(g):
-        return fast if g < FAST else slow
+        return rows
 
     fetch_all(plan, where)
 
@@ -361,46 +341,52 @@
         return places + [below + j for j in range(2 * HALO) if 0 <= below + j < HALO + LEND]
 
     clear(fields, vector, HEAD_BLANK, blank_places)
+    for i in range(HEAD_BLANK):
+        vector[0][i] = with_ones(jnp.zeros((COMPS, TILE), F32))
     for shift, part in enumerate((own, near, far, opposite)):
         g = lax.rem(group[0] + 4 - shift, 4)
         surface[:, pl.ds(pl.multiple_of(g * SUB, SUB), SUB)] = part[...]
         for j in range(HALO):
-            value = part[:, j * TILE : (j + 1) * TILE]
-            i = g * HALO + j
-            new = value / (CENTRE * diag[i])
-            residual[LEND + i] = value
-            direction[LEND + i] = new
-            total[LEND + i] = new
-            vector[0][HALO + LEND + i] = with_ones(new)
-    advance(plan, where, LEND, strengths(group[0]), vector, direction, residual, total)
-
-
-def second_kernel(plan, table, lent_table, place, group, film, heat, facts, vectors_in, fields_in, fast_hbm,
-                  *rest):
-    lent_hbm, rest = rest[: len(PIECES)], rest[len(PIECES) :]
-    head, edge, vectors, fields, fast_buffer, lent_buffer, sems = rest
+            residual[LEND + g * HALO + j] = part[:, j * TILE : (j + 1) * TILE]
+    products = []
+    for g in range(SURF_TILES // HALO):
+        rows.wait(g)
+        for j in range(HALO):
+            products.append(rows.product(vector[0], g, j))
+            rows.turn(g, j)
+    for i, product in enumerate(products):
+        new = residual[LEND + i] / (CENTRE * rows.diagonal(product, i // HALO, i % HALO))
+        direction[LEND + i] = new
+        total[LEND + i] = new
+        vector[0][HALO + LEND + i] = with_ones(new)
+    rows.ready.update(range(SURF_TILES // HALO))
+    advance(plan, where, LEND, strengths(group[0]), vector, direction, residual, total, range(FAST))
+
+
+def second_kernel(plan, table, facts_scalars, place, group, film, heat, facts, vectors_in, fields_in, turned,
+                  far_hbm, near_hbm, head, edge, vectors, fields, buffer, sems):
+    del vectors_in, fields_in
     vector, direction, residual, total = split((vectors, fields), HEAD_ROWS)
     first = (place[0] == 0).astype(F32)
-    lent_groups = range(-LEND // HALO, 0)
+
+    class LentTable:
+        def __getitem__(self, index):
+            return facts_scalars[index].astype(jnp.int32)
 
     def lent_rows(g):
         row = HALO * g + LEND
-        for piece, count in zip(lent_hbm, PIECES):
-            if row < count:
-                return piece.at[pl.ds(row, HALO)]
-            row -= count
-
-    lent = Rows(lent_groups, FAST, False, lent_rows, lent_buffer, sems, lent_table,
-                facts.at[pl.ds(SLOTS, LEND)], facts.at[pl.ds(SLOTS + LEND, LEND)], LEND,
-                table.shape[1], first)
-    fast = Rows(range(FAST), 0, True, rows_from(fast_hbm, 0), fast_buffer, sems, table, film, heat, 0, 0)
+        ref, row = (far_hbm, row) if row < AHEAD else (near_hbm, row - AHEAD)
+        return ref.at[pl.ds(row, HALO)]
+
+    lent = Rows(range(-LEND // HALO, 0), LentTable(), facts.at[pl.ds(SLOTS, LEND)],
+                facts.at[pl.ds(SLOTS + LEND, LEND)], LEND, table.shape[1], first, source=lent_rows,
+                buffer=buffer, sems=sems)
+    fast = Rows((), table, film, heat, 0, 0, turned=turned, turned_groups=range(FAST), ready=range(FAST))
 
     def where(g):
         return lent if g < 0 else fast
 
     fetch_all(plan, where)
-    vectors[...] = vectors_in[...]
-    fields[...] = fields_in[...]
     advance(plan, where, LEND, strengths(group[0]), vector, direction, residual, total)
     for k in range(0, STEPS, 2):
         for j in range(HALO):
@@ -412,12 +398,14 @@
         head[:, j * TILE : (j + 1) * TILE] = total[LEND + j]
 
 
-def tail_kernel(plan, table, group, edge, film, heat, head, tiles_hbm, out, vectors, fields, buffer, sems):
+def tail_kernel(plan, table, group, edge, film, heat, head, tiles_hbm, out, vectors, fields, buffer, turned,
+                sems):
     vector, direction, residual, total = split((vectors, fields), TAIL)
     row_tiles = out.shape[1] // TILE
     first = row_tiles - TAIL
-    rows = Rows(range(-TAIL // HALO, 0), 0, False, rows_from(tiles_hbm, row_tiles), buffer, sems, table, film, heat,
-                row_tiles, row_tiles)
+    groups = range(-TAIL // HALO, 0)
+    rows = Rows(groups, table, film, heat, row_tiles, row_tiles, source=rows_from(tiles_hbm, row_tiles),
+                buffer=buffer, sems=sems, turned=turned, turned_groups=groups[1:])
 
     def where(g):
         return rows
@@ -495,16 +483,18 @@
     def array(shape, dtype=F32):
         return jax.ShapeDtypeStruct(shape, dtype)
 
-    packed, head_table, tail_table, facts = pl.pallas_call(
+    packed, head_table, tail_table, facts, far = pl.pallas_call(
         pack_kernel,
         out_shape=(
-            array((parts, PACK, TILE), BF16),
-            array((SLOTS, row_tiles), jnp.int32),
-            array((SLOTS, row_tiles), jnp.int32),
-            array((SLOTS + 2 * LEND, TILE)),
+            pltpu.HBM((parts, PACK, TILE), BF16),
+            pltpu.HBM((SLOTS, row_tiles), jnp.int32),
+            pltpu.HBM((SLOTS, row_tiles), jnp.int32),
+            pltpu.HBM((SLOTS + 2 * LEND, TILE), F32),
+            pltpu.HBM((AHEAD, SLOTS, TILE, TILE), BF16),
         ),
-        in_specs=[smem()] + [vmem()] * 7,
-        out_specs=(vmem(),) * 4,
+        in_specs=[smem()] + [vmem()] * 7 + [hbm()],
+        out_specs=(vmem(),) * 5,
+        scratch_shapes=[pltpu.SemaphoreType.DMA((AHEAD,))],
         compiler_params=kernel_params(8),
         name="pack",
     )(
@@ -513,52 +503,31 @@
             boundary_power_density,
             face_scales.reshape(parts, TILE),
             face_node.reshape(parts, TILE),
+            mask,
             columns,
-            mask,
             film,
             heat,
         ),
+        tile_values,
     )
     got = lax.all_to_all(packed, "space", 0, 0)
 
-    facts = lax.ppermute(facts, "space", up)
-    lent = pl.pallas_call(
+    near = pl.pallas_call(
         lend_kernel,
-        out_shape=[array((count, SLOTS, TILE, TILE), BF16) for count in PIECES],
+        out_shape=array((LEND - AHEAD, SLOTS, TILE, TILE), BF16),
         in_specs=[hbm()],
-        out_specs=[vmem()] * len(PIECES),
-        scratch_shapes=[pltpu.SemaphoreType.DMA((len(PIECES),))],
+        out_specs=vmem(),
+        scratch_shapes=[pltpu.SemaphoreType.DMA((LEND - AHEAD,))],
         compiler_params=kernel_params(8),
         cost_estimate=pl.CostEstimate(flops=0, bytes_accessed=6 << 20, transcendentals=0),
         name="lend",
     )(tile_values)
-    lent = [lax.ppermute(piece, "space", up) for piece in lent]
-    lent_table = facts[:SLOTS].astype(jnp.int32)
-
-    depth = 4
-    fast_tiles, diag = pl.pallas_call(
-        prep_kernel,
-        out_shape=(
-            pltpu.HBM((FAST * HALO, SLOTS, TILE, TILE), BF16),
-            array((SURF_TILES, COMPS, TILE)),
-        ),
-        in_specs=[smem(), vmem(), hbm()],
-        out_specs=(hbm(), vmem()),
-        scratch_shapes=[
-            pltpu.VMEM((depth, HALO, SLOTS, TILE, TILE), BF16),
-            pltpu.VMEM((FAST * HALO, SLOTS, TILE, TILE), BF16),
-            pltpu.SemaphoreType.DMA((depth,)),
-            pltpu.SemaphoreType.DMA((FAST,)),
-        ],
-        compiler_params=kernel_params(16),
-        cost_estimate=pl.CostEstimate(flops=0, bytes_accessed=12 << 20, transcendentals=0),
-        name="prep",
-    )(mask, film, tile_values)
-
-    (fast_tiles,) = in_hbm(fast_tiles)
+    far, near = (lax.ppermute(piece, "space", up) for piece in (far, near))
+    facts = lax.ppermute(facts, "space", up)
+
     parts_of = pl.pallas_call(
         scatter_kernel,
-        out_shape=(array((COMPS, SUB)),) * groups,
+        out_shape=(pltpu.HBM((COMPS, SUB), F32),) * groups,
         in_specs=[smem(), vmem(), vmem()],
         out_specs=(vmem(),) * groups,
         scratch_shapes=[pltpu.VMEM((LEVELS, SUB), F32)] * 2,
@@ -576,48 +545,59 @@
     def tile_buffer(count):
         return pltpu.VMEM((count * HALO, SLOTS, TILE, TILE), BF16)
 
-    surface, *state = pl.pallas_call(
+    held_shape = [pltpu.VMEM(*h) for h in held]
+    surface, *state, turned = pl.pallas_call(
         lambda *refs: first_kernel(first_plan, *refs),
-        out_shape=(array((COMPS, SURF_TILES * TILE)), *[array(*h) for h in held]),
-        in_specs=[smem()] * 2 + [vmem()] * 7 + [hbm()] * 2,
-        out_specs=(vmem(),) * 3,
+        out_shape=(
+            array((COMPS, SURF_TILES * TILE)),
+            *held_shape,
+            pltpu.VMEM((TURNED * HALO, SLOTS, TILE, TILE), BF16),
+        ),
+        in_specs=[smem()] * 2 + [vmem()] * 6 + [hbm(), pl.BlockSpec(memory_space=pl.ANY)],
+        out_specs=(vmem(),) * 4,
         scratch_shapes=[
-            tile_buffer(FAST),
-            tile_buffer(groups_here - FAST),
+            tile_buffer(groups_here),
             pltpu.SemaphoreType.DMA((groups_here,)),
         ],
         compiler_params=kernel_params(24),
-        cost_estimate=work(200),
+        cost_estimate=work(20),
         name="first",
-    )(head_table, group, *mixed, diag, film, heat, fast_tiles, tile_values)
-
-    head, edge = pl.pallas_call(
+    )(
+        *in_hbm(head_table),
+        group,
+        *mixed,
+        *in_hbm(film, heat),
+        tile_values,
+        far,
+    )
+
+    head, edge, *_ = pl.pallas_call(
         lambda *refs: second_kernel(second_plan, *refs),
         out_shape=(
             array((COMPS, HEAD * TILE)),
             array(((STEPS + 1) // 2, HALO, 2 * COMPS, TILE), BF16),
+            *held_shape,
         ),
-        in_specs=[smem()] * 4 + [vmem()] * 5 + [hbm()] * (1 + len(PIECES)),
-        out_specs=(vmem(),) * 2,
+        in_specs=[smem()] * 4 + [vmem()] * 6 + [pl.BlockSpec(memory_space=pl.ANY)] * 2,
+        out_specs=(vmem(),) * 4,
         scratch_shapes=[
-            *[pltpu.VMEM(*h) for h in held],
-            tile_buffer(FAST),
             tile_buffer(LEND // HALO),
-            pltpu.SemaphoreType.DMA((FAST + LEND // HALO,)),
+            pltpu.SemaphoreType.DMA((LEND // HALO,)),
         ],
-        compiler_params=kernel_params(24),
+        input_output_aliases={7: 2, 8: 3},
+        compiler_params=kernel_params(16),
         name="second",
     )(
         head_table,
-        lent_table,
+        facts,
         place.astype(jnp.int32).reshape(1),
         group,
         film,
         heat,
         facts,
-        *state,
-        fast_tiles,
-        *lent,
+        *[pltpu.with_memory_space_constraint(x, pltpu.VMEM) for x in (*state, turned)],
+        far,
+        near,
     )
     edge = lax.ppermute(edge, "space", down)
 
@@ -629,6 +609,7 @@
         scratch_shapes=[
             *[pltpu.VMEM(*h) for h in state_shape(TAIL)],
             tile_buffer(TAIL // HALO),
+            tile_buffer(TAIL // HALO - 1),
             pltpu.SemaphoreType.DMA((TAIL // HALO,)),
         ],
         compiler_params=kernel_params(24),

time: 84.4 us -> 78.4 us (0.929)
  Pallas kernels: 46.4 us -> 37.5 us
  starting transfers between devices: 21.6 us -> 26 us
  waiting for transfers between devices: 14.3 us -> 12.1 us
    ppermute x1 -> x2, waiting for transfers between devices: 7.54 us -> 0.01 us  [local(): far, near = (lax.ppermute(piece, 'space', up) for piece in (far, near))]
    pallas_call x4 -> x3, Pallas kernels: 13.8 us -> 7.5 us  [the longest x1 3.37 us: local(): pl.pallas_call(pack_kernel, out_shape=(pltpu.HBM((parts, PACK, TILE), BF1...]
    all_to_all x1, waiting for transfers between devices: 0.01 us -> 6.32 us  [local(): got = lax.all_to_all(packed, 'space', 0, 0)]
    ppermute x1 -> x2, starting transfers between devices: 2.06 us -> 5.65 us  [local(): far, near = (lax.ppermute(piece, 'space', up) for piece in (far, near))]
    pallas_call x1, Pallas kernels: 11.2 us -> 8.7 us  [local(): pl.pallas_call(lambda *refs: tail_kernel(tail_plan(), *refs), out_shape=a...]
    ppermute x3, waiting for transfers between devices: 1.91 us -> 0.01 us  [local(): lax.ppermute(parts_of[s], 'freq', [(i, (i + s) % groups) for i in range(g...]
    ppermute x1, starting transfers between devices: 3.47 us -> 5.2 us  [local(): facts = lax.ppermute(facts, 'space', up)]
    ppermute x1, starting transfers between devices: 3.54 us -> 1.92 us  [local(): edge = lax.ppermute(edge, 'space', down)]
  transfers between devices with their start and end apart: 7 -> 8, of which waited for: 4 -> 2; matrix products, arithmetic and copies ran while one was open for 0% -> 0% of each run, Pallas kernels for 28% -> 21%
where the time goes in v3:
time: 78.4 us; the launch traced here: 77.9 us
  Pallas kernels  37.5 us (48%)
  starting transfers between devices  26 us (33%)
  waiting for transfers between devices  12.1 us (15%)
  local copies, waits for them, and re-layouts  1.38 us (2%)
  between operations  0.97 us (1%)
    pallas_call x1, Pallas kernels, local(): pl.pallas_call(lambda *refs: first_kernel(first_plan, *refs), out_shape=(...  12 us
    pallas_call x1, Pallas kernels, local(): pl.pallas_call(lambda *refs: second_kernel(second_plan, *refs), out_shape...  9.27 us
    pallas_call x1, Pallas kernels, local(): pl.pallas_call(lambda *refs: tail_kernel(tail_plan(), *refs), out_shape=a...  8.7 us
    all_to_all x1, starting transfers between devices, local(): got = lax.all_to_all(packed, 'space', 0, 0)  8.23 us
    all_to_all x1, waiting for transfers between devices, local(): got = lax.all_to_all(packed, 'space', 0, 0)  6.32 us
    ppermute x1, waiting for transfers between devices, local(): edge = lax.ppermute(edge, 'space', down)  5.77 us
    ppermute x2, starting transfers between devices, local(): far, near = (lax.ppermute(piece, 'space', up) for piece in (far, near))  5.65 us
    ppermute x1, starting transfers between devices, local(): facts = lax.ppermute(facts, 'space', up)  5.2 us
  transfers between devices with their start and end apart: 8, of which 2 were waited for; matrix products, arithmetic and copies ran while one was open for 0% of the time, Pallas kernels for 21%

profile of v3, /device:TPU:97, one launch (start us, length us, event | category | flops | bytes accessed | tf_op | source)
XLA Modules:
  0.0 77.9 jit_solution(9767327038964049433)
XLA Ops:
  0.6 0.0 copy-start.5
  0.6 0.6 copy-done.5
  1.3 3.4 %pack.1 = (bf16[32,48,128]{2,1,0:T(8,128)(2,1)}, s32[8,128]{1,0:T(8,128)}, s32[8,128]{1,0:T(8,128)}, f32[32,128]{1,0:T(8,128)}, bf16[4,8,128,128]{3,2,1,0:T(8,128)(2,1)}) custom-call(s32[32]{0:T(128)S(1)} %copy-done.5, bf16[32,4096]{1,0:T(8,128)(2,1)} %power.1, bf16[32,128]{1,0:T(8,128)(2,1)} %bitcast.17, s32[32,128]{1,0:T(8,128)} %bitcast.16, ...), custom_call_target="tpu_custom_call" | custom-call | tf_op jit(solution)/shard_map/pack/pallas_call | solution.py:486
  4.7 2.3 %collective-permute-start.3 = (bf16[4,8,128,128]{3,2,1,0:T(8,128)(2,1)}, bf16[4,8,128,128]{3,2,1,0:T(8,128)(2,1)S(1)}, u32[]{:S(2)}, u32[]{:S(2)}) collective-permute-start(bf16[4,8,128,128]{3,2,1,0:T(8,128)(2,1)} %get-tuple-element.23), channel_id=1, source_target_pairs={{0,1},{1,2},{2,3},{3,4},{4,5},{5,6},{6,7},{7,8},{8,9},{9,10},{10,1... | collective-permute-start | bytes 3145736 | tf_op jit(solution)/shard_map/ppermute | solution.py:525
  7.0 8.2 %all-to-all-start = ((bf16[32,48,128]{2,1,0:T(8,128)(2,1)}), bf16[32,48,128]{2,1,0:T(8,128)(2,1)S(1)}, u32[]{:S(2)}, u32[]{:S(2)}) async-start(bf16[32,48,128]{2,1,0:T(8,128)(2,1)} %get-tuple-element.18), calls=%async_computation | async-start | bytes 786432 | tf_op jit(solution)/shard_map/all_to_all | solution.py:513
  15.2 0.0 copy-start.2
  15.2 1.6 %lend.1 = bf16[8,8,128,128]{3,2,1,0:T(8,128)(2,1)S(1)} custom-call(bf16[128,8,128,128]{3,2,1,0:T(8,128)(2,1)} %refs_6_.1), custom_call_target="tpu_custom_call" | custom-call | bytes 6291456 | tf_op jit(solution)/shard_map/lend/pallas_call | solution.py:515
  16.8 3.3 %collective-permute-start.5 = (bf16[8,8,128,128]{3,2,1,0:T(8,128)(2,1)S(1)}, bf16[8,8,128,128]{3,2,1,0:T(8,128)(2,1)}, u32[]{:S(2)}, u32[]{:S(2)}) collective-permute-start(bf16[8,8,128,128]{3,2,1,0:T(8,128)(2,1)S(1)} %lend.1), channel_id=1, source_target_pairs={{0,1},{1,2},{2,3},{3,4},{4,5},{5,6},{6,7},{7,8},{8,9},{9,10},{10,1... | collective-permute-start | bytes 6291464 | tf_op jit(solution)/shard_map/ppermute | solution.py:525
  20.2 6.3 %all-to-all-done.got = bf16[32,48,128]{2,1,0:T(8,128)(2,1)S(1)} async-done(((bf16[32,48,128]{2,1,0:T(8,128)(2,1)}), bf16[32,48,128]{2,1,0:T(8,128)(2,1)S(1)}, u32[]{:S(2)}, u32[]{:S(2)}) %all-to-all-start) | async-done | bytes 393248 | tf_op jit(solution)/shard_map/all_to_all | solution.py:513
  26.5 0.0 copy-done.2
  26.5 2.6 %scatter.1 = (f32[8,512]{1,0:T(8,128)}, f32[8,512]{1,0:T(8,128)}, f32[8,512]{1,0:T(8,128)}, f32[8,512]{1,0:T(8,128)}) custom-call(s32[1]{0:T(128)} %bitcast.6.group.refs_1_.refs_3_, f32[32,32]{1,0:T(8,128)S(1)} %copy-done.2, bf16[32,48,128]{2,1,0:T(8,128)(2,1)S(1)} %all-to-all-done.got), custom_call_target="tpu_custom_call" | custom-call | tf_op jit(solution)/shard_map/scatter/pallas_call | solution.py:528
  29.1 1.3 %collective-permute-start = (f32[8,512]{1,0:T(8,128)}, f32[8,512]{1,0:T(8,128)S(1)}, u32[]{:S(2)}, u32[]{:S(2)}) collective-permute-start(f32[8,512]{1,0:T(8,128)} %get-tuple-element.20), channel_id=1, source_target_pairs={{0,32},{32,64},{64,96},{96,0},{1,33},{33,65},{65,97},{97,1},{2,34}... | collective-permute-start | bytes 49160 | tf_op jit(solution)/shard_map/ppermute | solution.py:538
  30.4 2.6 %collective-permute-start.1 = (f32[8,512]{1,0:T(8,128)}, f32[8,512]{1,0:T(8,128)S(1)}, u32[]{:S(2)}, u32[]{:S(2)}) collective-permute-start(f32[8,512]{1,0:T(8,128)} %get-tuple-element.21), channel_id=1, source_target_pairs={{0,64},{32,96},{64,0},{96,32},{1,65},{33,97},{65,1},{97,33},{2,66}... | collective-permute-start | bytes 49160 | tf_op jit(solution)/shard_map/ppermute | solution.py:538
  33.0 1.1 %collective-permute-start.2 = (f32[8,512]{1,0:T(8,128)}, f32[8,512]{1,0:T(8,128)S(1)}, u32[]{:S(2)}, u32[]{:S(2)}) collective-permute-start(f32[8,512]{1,0:T(8,128)} %get-tuple-element.22), channel_id=1, source_target_pairs={{0,96},{32,0},{64,32},{96,64},{1,97},{33,1},{65,33},{97,65},{2,98}... | collective-permute-start | bytes 49160 | tf_op jit(solution)/shard_map/ppermute | solution.py:538
  34.0 0.0 collective-permute-done.refs_3_
  34.0 5.2 %collective-permute-start.4 = (f32[32,128]{1,0:T(8,128)}, f32[32,128]{1,0:T(8,128)S(1)}, u32[]{:S(2)}, u32[]{:S(2)}) collective-permute-start(f32[32,128]{1,0:T(8,128)} %get-tuple-element.26), channel_id=1, source_target_pairs={{0,1},{1,2},{2,3},{3,4},{4,5},{5,6},{6,7},{7,8},{8,9},{9,10},{10,1... | collective-permute-start | bytes 49160 | tf_op jit(solution)/shard_map/ppermute | solution.py:526
  39.3 0.0 collective-permute-done.1.refs_4_
  39.3 0.0 collective-permute-done.2.refs_5_
  39.3 0.0 collective-permute-done.3.refs_9_.refs_10_
  39.3 0.0 copy-start.6
  39.3 0.7 copy-done.6
  40.0 0.0 copy-start
  40.0 0.0 copy-start.1
  40.0 0.0 copy-start.3
  40.0 12.0 %first.1 = (f32[8,2048]{1,0:T(8,128)}, bf16[455,16,128]{2,1,0:T(8,128)(2,1)S(1)}, f32[168,8,128]{2,1,0:T(8,128)S(1)}, bf16[36,8,128,128]{3,2,1,0:T(8,128)(2,1)S(1)}) custom-call(s32[8,128]{1,0:T(8,128)} %get-tuple-element.17.refs_0_, s32[1]{0:T(128)} %bitcast.6.group.refs_1_.refs_3_, f32[8,512]{1,0:T(8,128)S(1)} %copy-done.6, ...), custom_call_target="tpu_custom_call" | custom-call | flops 20000000000 | tf_op jit(solution)/shard_map/first/pallas_call | solution.py:549
  52.0 0.0 collective-permute-done.4.refs_1_.refs_6_
  52.0 0.0 collective-permute-done.5.refs_11_
  52.1 0.0 copy-done
  52.1 0.0 copy-done.1
  52.1 0.0 copy-done.3
  52.1 0.0 copy-start.4
  52.1 9.3 %second.1 = (f32[8,5632]{1,0:T(8,128)S(1)}, bf16[4,4,16,128]{3,2,1,0:T(8,128)(2,1)S(1)}, bf16[455,16,128]{2,1,0:T(8,128)(2,1)S(1)}, f32[168,8,128]{2,1,0:T(8,128)S(1)}) custom-call(s32[8,128]{1,0:T(8,128)S(1)} %copy-done.3, f32[32,128]{1,0:T(8,128)S(1)} %collective-permute-done.4.refs_1_.refs_6_, ...), custom_call_target="tpu_custom_call", output_to_operand_aliasing={{2}: (7, {}), {3}: (8, {})} | custom-call | tf_op jit(solution)/shard_map/second/pallas_call | solution.py:574
  61.4 1.9 %collective-permute-start.6 = (bf16[4,4,16,128]{3,2,1,0:T(8,128)(2,1)S(1)}, bf16[4,4,16,128]{3,2,1,0:T(8,128)(2,1)S(1)}, u32[]{:S(2)}, u32[]{:S(2)}) collective-permute-start(bf16[4,4,16,128]{3,2,1,0:T(8,128)(2,1)S(1)} %get-tuple-element.30), channel_id=1, source_target_pairs={{1,0},{2,1},{3,2},{4,3},{5,4},{6,5},{7,6},{8,7},{9,8},{10,9},{11,1... | collective-permute-start | bytes 196616 | tf_op jit(solution)/shard_map/ppermute | solution.py:602
  63.3 5.8 %collective-permute-done.6.refs_2_ = bf16[4,4,16,128]{3,2,1,0:T(8,128)(2,1)S(1)} collective-permute-done((bf16[4,4,16,128]{3,2,1,0:T(8,128)(2,1)S(1)}, bf16[4,4,16,128]{3,2,1,0:T(8,128)(2,1)S(1)}, u32[]{:S(2)}, u32[]{:S(2)}) %collective-permute-start.6) | collective-permute-done | bytes 65568 | tf_op jit(solution)/shard_map/ppermute | solution.py:602
  69.1 0.0 copy-done.4
  69.1 8.7 %tail.1 = f32[8,16384]{1,0:T(8,128)} custom-call(s32[8,128]{1,0:T(8,128)S(1)} %copy-done.4, s32[1]{0:T(128)} %bitcast.6.group.refs_1_.refs_3_, bf16[4,4,16,128]{3,2,1,0:T(8,128)(2,1)S(1)} %collective-permute-done.6.refs_2_, f32[128,128]{1,0:T(8,128)S(1)} %bitcast.11, f32[128,128]{1,0:T(8,128)S(1)} %bitcast.15, f32[8,5632]{1,0:T(8,128)S(1)} %get-tuple-element.31.refs_5_, ...), custom_call_target="tpu_custom_call" | custom-call | tf_op jit(solution)/shard_map/tail/pallas_call | solution.py:604
Async XLA Ops:
  0.6 0.7 copy-start.5
  4.7 34.6 %collective-permute-start.3 = (bf16[4,8,128,128]{3,2,1,0:T(8,128)(2,1)}, bf16[4,8,128,128]{3,2,1,0:T(8,128)(2,1)S(1)}, u32[]{:S(2)}, u32[]{:S(2)}) collective-permute-start(bf16[4,8,128,128]{3,2,1,0:T(8,128)(2,1)} %get-tuple-element.23), channel_id=1, source_target_pairs={{0,1},{1,2},{2,3},{3,4},{4,5},{5,6},{6,7},{7,8},{8,9},{9,10},{10,1... | collective-permute-start | bytes 3145736 | tf_op jit(solution)/shard_map/ppermute | solution.py:525
  7.0 19.5 %all-to-all-start = ((bf16[32,48,128]{2,1,0:T(8,128)(2,1)}), bf16[32,48,128]{2,1,0:T(8,128)(2,1)S(1)}, u32[]{:S(2)}, u32[]{:S(2)}) async-start(bf16[32,48,128]{2,1,0:T(8,128)(2,1)} %get-tuple-element.18), calls=%async_computation | async-start | bytes 786432 | tf_op jit(solution)/shard_map/all_to_all | solution.py:513
  15.2 11.3 %copy-start.2 = (f32[32,32]{1,0:T(8,128)S(1)}, f32[32,32]{1,0:T(8,128)}, u32[]{:S(2)}) copy-start(f32[32,32]{1,0:T(8,128)} %constant.11.clone.table) | copy-start | bytes 12292
  16.8 35.2 %collective-permute-start.5 = (bf16[8,8,128,128]{3,2,1,0:T(8,128)(2,1)S(1)}, bf16[8,8,128,128]{3,2,1,0:T(8,128)(2,1)}, u32[]{:S(2)}, u32[]{:S(2)}) collective-permute-start(bf16[8,8,128,128]{3,2,1,0:T(8,128)(2,1)S(1)} %lend.1), channel_id=1, source_target_pairs={{0,1},{1,2},{2,3},{3,4},{4,5},{5,6},{6,7},{7,8},{8,9},{9,10},{10,1... | collective-permute-start | bytes 6291464 | tf_op jit(solution)/shard_map/ppermute | solution.py:525
  29.1 5.0 %collective-permute-start = (f32[8,512]{1,0:T(8,128)}, f32[8,512]{1,0:T(8,128)S(1)}, u32[]{:S(2)}, u32[]{:S(2)}) collective-permute-start(f32[8,512]{1,0:T(8,128)} %get-tuple-element.20), channel_id=1, source_target_pairs={{0,32},{32,64},{64,96},{96,0},{1,33},{33,65},{65,97},{97,1},{2,34}... | collective-permute-start | bytes 49160 | tf_op jit(solution)/shard_map/ppermute | solution.py:538
  30.4 8.9 %collective-permute-start.1 = (f32[8,512]{1,0:T(8,128)}, f32[8,512]{1,0:T(8,128)S(1)}, u32[]{:S(2)}, u32[]{:S(2)}) collective-permute-start(f32[8,512]{1,0:T(8,128)} %get-tuple-element.21), channel_id=1, source_target_pairs={{0,64},{32,96},{64,0},{96,32},{1,65},{33,97},{65,1},{97,33},{2,66}... | collective-permute-start | bytes 49160 | tf_op jit(solution)/shard_map/ppermute | solution.py:538
  33.0 6.3 %collective-permute-start.2 = (f32[8,512]{1,0:T(8,128)}, f32[8,512]{1,0:T(8,128)S(1)}, u32[]{:S(2)}, u32[]{:S(2)}) collective-permute-start(f32[8,512]{1,0:T(8,128)} %get-tuple-element.22), channel_id=1, source_target_pairs={{0,96},{32,0},{64,32},{96,64},{1,97},{33,1},{65,33},{97,65},{2,98}... | collective-permute-start | bytes 49160 | tf_op jit(solution)/shard_map/ppermute | solution.py:538
  34.0 18.0 %collective-permute-start.4 = (f32[32,128]{1,0:T(8,128)}, f32[32,128]{1,0:T(8,128)S(1)}, u32[]{:S(2)}, u32[]{:S(2)}) collective-permute-start(f32[32,128]{1,0:T(8,128)} %get-tuple-element.26), channel_id=1, source_target_pairs={{0,1},{1,2},{2,3},{3,4},{4,5},{5,6},{6,7},{7,8},{8,9},{9,10},{10,1... | collective-permute-start | bytes 49160 | tf_op jit(solution)/shard_map/ppermute | solution.py:526
  39.3 0.7 copy-start.6
  40.0 12.1 %copy-start = (f32[16384]{0:T(1024)S(1)}, f32[16384]{0:T(1024)}, u32[]{:S(2)}) copy-start(f32[16384]{0:T(1024)} %param.17) | copy-start | bytes 196612
  40.0 12.1 %copy-start.1 = (f32[16384]{0:T(1024)S(1)}, f32[16384]{0:T(1024)}, u32[]{:S(2)}) copy-start(f32[16384]{0:T(1024)} %param.18) | copy-start | bytes 196612
  40.0 12.1 %copy-start.3 = (s32[8,128]{1,0:T(8,128)S(1)}, s32[8,128]{1,0:T(8,128)}, u32[]{:S(2)}) copy-start(s32[8,128]{1,0:T(8,128)} %get-tuple-element.17.refs_0_) | copy-start | bytes 12292
  52.1 17.0 %copy-start.4 = (s32[8,128]{1,0:T(8,128)S(1)}, s32[8,128]{1,0:T(8,128)}, u32[]{:S(2)}) copy-start(s32[8,128]{1,0:T(8,128)} %get-tuple-element.25.refs_0_) | copy-start | bytes 12292
  61.4 7.7 %collective-permute-start.6 = (bf16[4,4,16,128]{3,2,1,0:T(8,128)(2,1)S(1)}, bf16[4,4,16,128]{3,2,1,0:T(8,128)(2,1)S(1)}, u32[]{:S(2)}, u32[]{:S(2)}) collective-permute-start(bf16[4,4,16,128]{3,2,1,0:T(8,128)(2,1)S(1)} %get-tuple-element.30), channel_id=1, source_target_pairs={{1,0},{2,1},{3,2},{4,3},{5,4},{6,5},{7,6},{8,7},{9,8},{10,9},{11,1... | collective-permute-start | bytes 196616 | tf_op jit(solution)/shard_map/ppermute | solution.py:602

commit v4 on v3

--- a/solution.py
+++ b/solution.py
@@ -103,7 +103,8 @@
     return copies
 
 
-def lend_kernel(tiles_hbm, near, sems):
+def lend_kernel(tiles_hbm, after, near, sems):
+    del after
     for copy in copy_rows(tiles_hbm, tiles_hbm.shape[0] - LEND + AHEAD, near, sems):
         copy.wait()
 
@@ -512,18 +513,18 @@
     )
     got = lax.all_to_all(packed, "space", 0, 0)
 
+    facts = lax.ppermute(facts, "space", up)
     near = pl.pallas_call(
         lend_kernel,
         out_shape=array((LEND - AHEAD, SLOTS, TILE, TILE), BF16),
-        in_specs=[hbm()],
+        in_specs=[hbm(), pl.BlockSpec(memory_space=pl.ANY)],
         out_specs=vmem(),
         scratch_shapes=[pltpu.SemaphoreType.DMA((LEND - AHEAD,))],
         compiler_params=kernel_params(8),
         cost_estimate=pl.CostEstimate(flops=0, bytes_accessed=6 << 20, transcendentals=0),
         name="lend",
-    )(tile_values)
+    )(tile_values, facts)
     far, near = (lax.ppermute(piece, "space", up) for piece in (far, near))
-    facts = lax.ppermute(facts, "space", up)
 
     parts_of = pl.pallas_call(
         scatter_kernel,

time: 78.4 us -> 82.1 us (1.047)
  waiting for transfers between devices: 12.1 us -> 13.8 us
  starting transfers between devices: 26 us -> 27.3 us
    all_to_all x1, waiting for transfers between devices: 6.32 us -> 0.01 us  [local(): got = lax.all_to_all(packed, 'space', 0, 0)]
    ppermute x1, waiting for transfers between devices: 0.01 us -> 5.25 us  [local(): facts = lax.ppermute(facts, 'space', up)]
    ppermute x2, starting transfers between devices: 5.65 us -> 8.81 us  [local(): far, near = (lax.ppermute(piece, 'space', up) for piece in (far, near))]
    ppermute x3, waiting for transfers between devices: 0.01 us -> 2.13 us  [local(): lax.ppermute(parts_of[s], 'freq', [(i, (i + s) % groups) for i in range(g...]
    ppermute x1, starting transfers between devices: 5.2 us -> 3.34 us  [local(): facts = lax.ppermute(facts, 'space', up)]
  transfers between devices with their start and end apart: 8 -> 8, of which waited for: 2 -> 4; matrix products, arithmetic and copies ran while one was open for 0% -> 0% of each run, Pallas kernels for 21% -> 20%
where the time goes in v4:
time: 82.1 us; the launch traced here: 81.6 us
  Pallas kernels  37.5 us (46%)
  starting transfers between devices  27.3 us (33%)
  waiting for transfers between devices  13.8 us (17%)
  local copies, waits for them, and re-layouts  2.1 us (3%)
  between operations  0.94 us (1%)
    pallas_call x1, Pallas kernels, local(): pl.pallas_call(lambda *refs: first_kernel(first_plan, *refs), out_shape=(...  12 us
    pallas_call x1, Pallas kernels, local(): pl.pallas_call(lambda *refs: second_kernel(second_plan, *refs), out_shape...  9.26 us
    ppermute x2, starting transfers between devices, local(): far, near = (lax.ppermute(piece, 'space', up) for piece in (far, near))  8.81 us
    pallas_call x1, Pallas kernels, local(): pl.pallas_call(lambda *refs: tail_kernel(tail_plan(), *refs), out_shape=a...  8.71 us
    all_to_all x1, starting transfers between devices, local(): got = lax.all_to_all(packed, 'space', 0, 0)  8.23 us
    ppermute x1, waiting for transfers between devices, local(): edge = lax.ppermute(edge, 'space', down)  6.38 us
    ppermute x1, waiting for transfers between devices, local(): facts = lax.ppermute(facts, 'space', up)  5.25 us
    ppermute x3, starting transfers between devices, local(): lax.ppermute(parts_of[s], 'freq', [(i, (i + s) % groups) for i in range(g...  4.99 us
  transfers between devices with their start and end apart: 8, of which 4 were waited for; matrix products, arithmetic and copies ran while one was open for 0% of the time, Pallas kernels for 20%

profile of v4, /device:TPU:97, one launch (start us, length us, event | category | flops | bytes accessed | tf_op | source)
XLA Modules:
  0.0 81.6 jit_solution(3739715144338220794)
XLA Ops:
  0.6 0.0 copy-start.5
  0.6 0.6 copy-done.5
  1.3 3.4 %pack.1 = (bf16[32,48,128]{2,1,0:T(8,128)(2,1)}, s32[8,128]{1,0:T(8,128)}, s32[8,128]{1,0:T(8,128)}, f32[32,128]{1,0:T(8,128)}, bf16[4,8,128,128]{3,2,1,0:T(8,128)(2,1)}) custom-call(s32[32]{0:T(128)S(1)} %copy-done.5, bf16[32,4096]{1,0:T(8,128)(2,1)} %power.1, bf16[32,128]{1,0:T(8,128)(2,1)} %bitcast.17, s32[32,128]{1,0:T(8,128)} %bitcast.16, ...), custom_call_target="tpu_custom_call" | custom-call | tf_op jit(solution)/shard_map/pack/pallas_call | solution.py:487
  4.7 2.3 %collective-permute-start.3 = (bf16[4,8,128,128]{3,2,1,0:T(8,128)(2,1)}, bf16[4,8,128,128]{3,2,1,0:T(8,128)(2,1)S(1)}, u32[]{:S(2)}, u32[]{:S(2)}) collective-permute-start(bf16[4,8,128,128]{3,2,1,0:T(8,128)(2,1)} %get-tuple-element.23), channel_id=1, source_target_pairs={{0,1},{1,2},{2,3},{3,4},{4,5},{5,6},{6,7},{7,8},{8,9},{9,10},{10,1... | collective-permute-start | bytes 3145736 | tf_op jit(solution)/shard_map/ppermute | solution.py:527
  7.0 8.2 %all-to-all-start = ((bf16[32,48,128]{2,1,0:T(8,128)(2,1)}), bf16[32,48,128]{2,1,0:T(8,128)(2,1)S(1)}, u32[]{:S(2)}, u32[]{:S(2)}) async-start(bf16[32,48,128]{2,1,0:T(8,128)(2,1)} %get-tuple-element.18), calls=%async_computation | async-start | bytes 786432 | tf_op jit(solution)/shard_map/all_to_all | solution.py:514
  15.2 3.3 %collective-permute-start.4 = (f32[32,128]{1,0:T(8,128)}, f32[32,128]{1,0:T(8,128)S(1)}, u32[]{:S(2)}, u32[]{:S(2)}) collective-permute-start(f32[32,128]{1,0:T(8,128)} %get-tuple-element.26), channel_id=1, source_target_pairs={{0,1},{1,2},{2,3},{3,4},{4,5},{5,6},{6,7},{7,8},{8,9},{9,10},{10,1... | collective-permute-start | bytes 49160 | tf_op jit(solution)/shard_map/ppermute | solution.py:516
  18.6 5.3 %collective-permute-done.4.after.refs_1_.refs_6_ = f32[32,128]{1,0:T(8,128)S(1)} collective-permute-done((f32[32,128]{1,0:T(8,128)}, f32[32,128]{1,0:T(8,128)S(1)}, u32[]{:S(2)}, u32[]{:S(2)}) %collective-permute-start.4) | collective-permute-done | bytes 16416 | tf_op jit(solution)/shard_map/ppermute | solution.py:516
  23.8 1.6 %lend.1 = bf16[8,8,128,128]{3,2,1,0:T(8,128)(2,1)S(1)} custom-call(bf16[128,8,128,128]{3,2,1,0:T(8,128)(2,1)} %refs_6_.1, f32[32,128]{1,0:T(8,128)S(1)} %collective-permute-done.4.after.refs_1_.refs_6_), custom_call_target="tpu_custom_call" | custom-call | bytes 6291456 | tf_op jit(solution)/shard_map/lend/pallas_call | solution.py:517
  25.4 6.5 %collective-permute-start.5 = (bf16[8,8,128,128]{3,2,1,0:T(8,128)(2,1)S(1)}, bf16[8,8,128,128]{3,2,1,0:T(8,128)(2,1)}, u32[]{:S(2)}, u32[]{:S(2)}) collective-permute-start(bf16[8,8,128,128]{3,2,1,0:T(8,128)(2,1)S(1)} %lend.1), channel_id=1, source_target_pairs={{0,1},{1,2},{2,3},{3,4},{4,5},{5,6},{6,7},{7,8},{8,9},{9,10},{10,1... | collective-permute-start | bytes 6291464 | tf_op jit(solution)/shard_map/ppermute | solution.py:527
  31.9 0.0 all-to-all-done.got
  31.9 0.0 copy-start.2
  31.9 0.7 copy-done.2
  32.6 2.5 %scatter.1 = (f32[8,512]{1,0:T(8,128)}, f32[8,512]{1,0:T(8,128)}, f32[8,512]{1,0:T(8,128)}, f32[8,512]{1,0:T(8,128)}) custom-call(s32[1]{0:T(128)} %bitcast.6.group.refs_1_.refs_3_, f32[32,32]{1,0:T(8,128)S(1)} %copy-done.2, bf16[32,48,128]{2,1,0:T(8,128)(2,1)S(1)} %all-to-all-done.got), custom_call_target="tpu_custom_call" | custom-call | tf_op jit(solution)/shard_map/scatter/pallas_call | solution.py:529
  35.2 1.3 %collective-permute-start = (f32[8,512]{1,0:T(8,128)}, f32[8,512]{1,0:T(8,128)S(1)}, u32[]{:S(2)}, u32[]{:S(2)}) collective-permute-start(f32[8,512]{1,0:T(8,128)} %get-tuple-element.20), channel_id=1, source_target_pairs={{0,32},{32,64},{64,96},{96,0},{1,33},{33,65},{65,97},{97,1},{2,34}... | collective-permute-start | bytes 49160 | tf_op jit(solution)/shard_map/ppermute | solution.py:539
  36.5 2.6 %collective-permute-start.1 = (f32[8,512]{1,0:T(8,128)}, f32[8,512]{1,0:T(8,128)S(1)}, u32[]{:S(2)}, u32[]{:S(2)}) collective-permute-start(f32[8,512]{1,0:T(8,128)} %get-tuple-element.21), channel_id=1, source_target_pairs={{0,64},{32,96},{64,0},{96,32},{1,65},{33,97},{65,1},{97,33},{2,66}... | collective-permute-start | bytes 49160 | tf_op jit(solution)/shard_map/ppermute | solution.py:539
  39.1 1.1 %collective-permute-start.2 = (f32[8,512]{1,0:T(8,128)}, f32[8,512]{1,0:T(8,128)S(1)}, u32[]{:S(2)}, u32[]{:S(2)}) collective-permute-start(f32[8,512]{1,0:T(8,128)} %get-tuple-element.22), channel_id=1, source_target_pairs={{0,96},{32,0},{64,32},{96,64},{1,97},{33,1},{65,33},{97,65},{2,98}... | collective-permute-start | bytes 49160 | tf_op jit(solution)/shard_map/ppermute | solution.py:539
  40.2 0.0 collective-permute-done.refs_3_
  40.2 0.6 collective-permute-done.1.refs_4_
  40.8 1.5 %collective-permute-done.2.refs_5_ = f32[8,512]{1,0:T(8,128)S(1)} collective-permute-done((f32[8,512]{1,0:T(8,128)}, f32[8,512]{1,0:T(8,128)S(1)}, u32[]{:S(2)}, u32[]{:S(2)}) %collective-permute-start.2) | collective-permute-done | bytes 16416 | tf_op jit(solution)/shard_map/ppermute | solution.py:539
  42.3 0.0 collective-permute-done.3.refs_9_.refs_10_
  42.3 0.0 copy-start.6
  42.3 0.7 copy-done.6
  43.0 0.0 copy-start
  43.0 0.0 copy-start.1
  43.0 0.0 copy-start.3
  43.0 12.0 %first.1 = (f32[8,2048]{1,0:T(8,128)}, bf16[455,16,128]{2,1,0:T(8,128)(2,1)S(1)}, f32[168,8,128]{2,1,0:T(8,128)S(1)}, bf16[36,8,128,128]{3,2,1,0:T(8,128)(2,1)S(1)}) custom-call(s32[8,128]{1,0:T(8,128)} %get-tuple-element.17.refs_0_, s32[1]{0:T(128)} %bitcast.6.group.refs_1_.refs_3_, f32[8,512]{1,0:T(8,128)S(1)} %copy-done.6, ...), custom_call_target="tpu_custom_call" | custom-call | flops 20000000000 | tf_op jit(solution)/shard_map/first/pallas_call | solution.py:550
  55.1 0.0 collective-permute-done.5.refs_11_
  55.1 0.0 copy-done
  55.1 0.0 copy-done.1
  55.1 0.0 copy-done.3
  55.1 0.0 copy-start.4
  55.1 9.3 %second.1 = (f32[8,5632]{1,0:T(8,128)S(1)}, bf16[4,4,16,128]{3,2,1,0:T(8,128)(2,1)S(1)}, bf16[455,16,128]{2,1,0:T(8,128)(2,1)S(1)}, f32[168,8,128]{2,1,0:T(8,128)S(1)}) custom-call(s32[8,128]{1,0:T(8,128)S(1)} %copy-done.3, f32[32,128]{1,0:T(8,128)S(1)} %collective-permute-done.4.after.refs_1_.refs_6_, ...), custom_call_target="tpu_custom_call", output_to_operand_aliasing={{2}: (7, {}), {3}: (8, {})} | custom-call | tf_op jit(solution)/shard_map/second/pallas_call | solution.py:575
  64.4 1.9 %collective-permute-start.6 = (bf16[4,4,16,128]{3,2,1,0:T(8,128)(2,1)S(1)}, bf16[4,4,16,128]{3,2,1,0:T(8,128)(2,1)S(1)}, u32[]{:S(2)}, u32[]{:S(2)}) collective-permute-start(bf16[4,4,16,128]{3,2,1,0:T(8,128)(2,1)S(1)} %get-tuple-element.30), channel_id=1, source_target_pairs={{1,0},{2,1},{3,2},{4,3},{5,4},{6,5},{7,6},{8,7},{9,8},{10,9},{11,1... | collective-permute-start | bytes 196616 | tf_op jit(solution)/shard_map/ppermute | solution.py:603
  66.3 6.4 %collective-permute-done.6.refs_2_ = bf16[4,4,16,128]{3,2,1,0:T(8,128)(2,1)S(1)} collective-permute-done((bf16[4,4,16,128]{3,2,1,0:T(8,128)(2,1)S(1)}, bf16[4,4,16,128]{3,2,1,0:T(8,128)(2,1)S(1)}, u32[]{:S(2)}, u32[]{:S(2)}) %collective-permute-start.6) | collective-permute-done | bytes 65568 | tf_op jit(solution)/shard_map/ppermute | solution.py:603
  72.7 0.0 copy-done.4
  72.7 8.7 %tail.1 = f32[8,16384]{1,0:T(8,128)} custom-call(s32[8,128]{1,0:T(8,128)S(1)} %copy-done.4, s32[1]{0:T(128)} %bitcast.6.group.refs_1_.refs_3_, bf16[4,4,16,128]{3,2,1,0:T(8,128)(2,1)S(1)} %collective-permute-done.6.refs_2_, f32[128,128]{1,0:T(8,128)S(1)} %bitcast.11, f32[128,128]{1,0:T(8,128)S(1)} %bitcast.15, f32[8,5632]{1,0:T(8,128)S(1)} %get-tuple-element.31.refs_5_, ...), custom_call_target="tpu_custom_call" | custom-call | tf_op jit(solution)/shard_map/tail/pallas_call | solution.py:605
Async XLA Ops:
  0.6 0.7 copy-start.5
  4.7 37.7 %collective-permute-start.3 = (bf16[4,8,128,128]{3,2,1,0:T(8,128)(2,1)}, bf16[4,8,128,128]{3,2,1,0:T(8,128)(2,1)S(1)}, u32[]{:S(2)}, u32[]{:S(2)}) collective-permute-start(bf16[4,8,128,128]{3,2,1,0:T(8,128)(2,1)} %get-tuple-element.23), channel_id=1, source_target_pairs={{0,1},{1,2},{2,3},{3,4},{4,5},{5,6},{6,7},{7,8},{8,9},{9,10},{10,1... | collective-permute-start | bytes 3145736 | tf_op jit(solution)/shard_map/ppermute | solution.py:527
  7.0 24.9 %all-to-all-start = ((bf16[32,48,128]{2,1,0:T(8,128)(2,1)}), bf16[32,48,128]{2,1,0:T(8,128)(2,1)S(1)}, u32[]{:S(2)}, u32[]{:S(2)}) async-start(bf16[32,48,128]{2,1,0:T(8,128)(2,1)} %get-tuple-element.18), calls=%async_computation | async-start | bytes 786432 | tf_op jit(solution)/shard_map/all_to_all | solution.py:514
  15.2 8.6 %collective-permute-start.4 = (f32[32,128]{1,0:T(8,128)}, f32[32,128]{1,0:T(8,128)S(1)}, u32[]{:S(2)}, u32[]{:S(2)}) collective-permute-start(f32[32,128]{1,0:T(8,128)} %get-tuple-element.26), channel_id=1, source_target_pairs={{0,1},{1,2},{2,3},{3,4},{4,5},{5,6},{6,7},{7,8},{8,9},{9,10},{10,1... | collective-permute-start | bytes 49160 | tf_op jit(solution)/shard_map/ppermute | solution.py:516
  25.4 29.7 %collective-permute-start.5 = (bf16[8,8,128,128]{3,2,1,0:T(8,128)(2,1)S(1)}, bf16[8,8,128,128]{3,2,1,0:T(8,128)(2,1)}, u32[]{:S(2)}, u32[]{:S(2)}) collective-permute-start(bf16[8,8,128,128]{3,2,1,0:T(8,128)(2,1)S(1)} %lend.1), channel_id=1, source_target_pairs={{0,1},{1,2},{2,3},{3,4},{4,5},{5,6},{6,7},{7,8},{8,9},{9,10},{10,1... | collective-permute-start | bytes 6291464 | tf_op jit(solution)/shard_map/ppermute | solution.py:527
  31.9 0.7 copy-start.2
  35.2 5.0 %collective-permute-start = (f32[8,512]{1,0:T(8,128)}, f32[8,512]{1,0:T(8,128)S(1)}, u32[]{:S(2)}, u32[]{:S(2)}) collective-permute-start(f32[8,512]{1,0:T(8,128)} %get-tuple-element.20), channel_id=1, source_target_pairs={{0,32},{32,64},{64,96},{96,0},{1,33},{33,65},{65,97},{97,1},{2,34}... | collective-permute-start | bytes 49160 | tf_op jit(solution)/shard_map/ppermute | solution.py:539
  36.5 4.3 %collective-permute-start.1 = (f32[8,512]{1,0:T(8,128)}, f32[8,512]{1,0:T(8,128)S(1)}, u32[]{:S(2)}, u32[]{:S(2)}) collective-permute-start(f32[8,512]{1,0:T(8,128)} %get-tuple-element.21), channel_id=1, source_target_pairs={{0,64},{32,96},{64,0},{96,32},{1,65},{33,97},{65,1},{97,33},{2,66}... | collective-permute-start | bytes 49160 | tf_op jit(solution)/shard_map/ppermute | solution.py:539
  39.1 3.2 %collective-permute-start.2 = (f32[8,512]{1,0:T(8,128)}, f32[8,512]{1,0:T(8,128)S(1)}, u32[]{:S(2)}, u32[]{:S(2)}) collective-permute-start(f32[8,512]{1,0:T(8,128)} %get-tuple-element.22), channel_id=1, source_target_pairs={{0,96},{32,0},{64,32},{96,64},{1,97},{33,1},{65,33},{97,65},{2,98}... | collective-permute-start | bytes 49160 | tf_op jit(solution)/shard_map/ppermute | solution.py:539
  42.3 0.7 copy-start.6
  43.0 12.0 %copy-start = (f32[16384]{0:T(1024)S(1)}, f32[16384]{0:T(1024)}, u32[]{:S(2)}) copy-start(f32[16384]{0:T(1024)} %param.17) | copy-start | bytes 196612
  43.0 12.0 %copy-start.1 = (f32[16384]{0:T(1024)S(1)}, f32[16384]{0:T(1024)}, u32[]{:S(2)}) copy-start(f32[16384]{0:T(1024)} %param.18) | copy-start | bytes 196612
  43.0 12.0 %copy-start.3 = (s32[8,128]{1,0:T(8,128)S(1)}, s32[8,128]{1,0:T(8,128)}, u32[]{:S(2)}) copy-start(s32[8,128]{1,0:T(8,128)} %get-tuple-element.17.refs_0_) | copy-start | bytes 12292
  55.1 17.6 %copy-start.4 = (s32[8,128]{1,0:T(8,128)S(1)}, s32[8,128]{1,0:T(8,128)}, u32[]{:S(2)}) copy-start(s32[8,128]{1,0:T(8,128)} %get-tuple-element.25.refs_0_) | copy-start | bytes 12292
  64.4 8.3 %collective-permute-start.6 = (bf16[4,4,16,128]{3,2,1,0:T(8,128)(2,1)S(1)}, bf16[4,4,16,128]{3,2,1,0:T(8,128)(2,1)S(1)}, u32[]{:S(2)}, u32[]{:S(2)}) collective-permute-start(bf16[4,4,16,128]{3,2,1,0:T(8,128)(2,1)S(1)} %get-tuple-element.30), channel_id=1, source_target_pairs={{1,0},{2,1},{3,2},{4,3},{5,4},{6,5},{7,6},{8,7},{9,8},{10,9},{11,1... | collective-permute-start | bytes 196616 | tf_op jit(solution)/shard_map/ppermute | solution.py:603
